TPU v7x, 32 devices: a whole 2x2x4 slice. The times are simulated.
32 devices in a mesh: ha: 8 (over z, core), wa: 4 (over y, x).
Axes of the slice: x: 2, y: 2, z: 4, core: 2. Of those that a mesh axis runs over, the one named last changes fastest.
Arguments:
- tokens: bfloat16 [128, 128, 512], P('ha', 'wa'), may hold values from -40 to 40
- cotangent: bfloat16 [128, 128, 512], P('ha', 'wa'), may hold values from -6 to 6
- norm_gain: float32 [512], replicated, may hold values from 0.1 to 1.9
- in_weight: bfloat16 [512, 1536], replicated, may hold values from -0.25 to 0.25
- out_weight: bfloat16 [512, 512], replicated, may hold values from -0.25 to 0.25
- bias_table: float32 [16, 31, 31], replicated, may hold values from -256 to 256
Outputs:
- grad_input: bfloat16 [128, 128, 512], P('ha', 'wa')
- grad_table: float32 [16, 31, 31], replicated
All inputs are finite; a program needn't handle non-finite values.
Results may differ from a plain program's by a relative error of at most 0.011.
Values may be sent and summed in bfloat16 or wider, within the bound.
A program may use at most 128 MiB of HBM per device.

v0:
```python
import jax
import jax.numpy as jnp
from jax import lax
from jax.sharding import PartitionSpec as P

D = 512
HEADS = 16
HEAD_DIM = 32
WIN = 16
TAB = 31


NORM_EPS = 1e-05


def offset_hot():
    places = jnp.arange(WIN)
    slot_ids = jnp.arange(TAB)
    return (
        places[:, None, None] - places[None, :, None] + (WIN - 1) == slot_ids[None, None, :]
    ).astype(jnp.float32)


def full_bias(bias_table, offset_table):
    partial_rows = jnp.einsum(
        "abd,hde->habe", offset_table, bias_table, precision=lax.Precision.HIGHEST
    )
    spread = jnp.einsum(
        "uve,habe->haubv", offset_table, partial_rows, precision=lax.Precision.HIGHEST
    )
    return spread.reshape(HEADS, WIN * WIN, WIN * WIN)


def group_grad(group_tokens, group_cot, norm_gain, in_weight, out_weight, bias_full, offset_table):
    group_rows = WIN * WIN
    tokens_wide = group_tokens.astype(jnp.float32)
    center = jnp.mean(tokens_wide, axis=-1, keepdims=True)
    shifted = tokens_wide - center
    inv_std = lax.rsqrt(jnp.mean(shifted * shifted, axis=-1, keepdims=True) + NORM_EPS)
    unit_rows = shifted * inv_std
    normed = (unit_rows * norm_gain).astype(jnp.bfloat16)
    mixed_rows = jnp.dot(normed, in_weight, preferred_element_type=jnp.float32)
    query_scale = HEAD_DIM ** (-0.5)
    queries = (
        (mixed_rows[:, :D] * query_scale).astype(jnp.bfloat16).reshape(group_rows, HEADS, HEAD_DIM)
    )
    key_rows = mixed_rows[:, D : 2 * D].astype(jnp.bfloat16).reshape(group_rows, HEADS, HEAD_DIM)
    values = mixed_rows[:, 2 * D :].astype(jnp.bfloat16).reshape(group_rows, HEADS, HEAD_DIM)
    scores = (
        jnp.einsum("thd,shd->hts", queries, key_rows, preferred_element_type=jnp.float32)
        + bias_full
    )
    row_top = jnp.max(scores, axis=-1, keepdims=True)
    exponent = jnp.exp(scores - row_top)
    attn_probs = exponent / jnp.sum(exponent, axis=-1, keepdims=True)
    probs_half = attn_probs.astype(jnp.bfloat16)
    grad_out = lax.dot_general(
        group_cot, out_weight, (((1,), (1,)), ((), ())), preferred_element_type=jnp.float32
    )
    grad_out = grad_out.astype(jnp.bfloat16).reshape(group_rows, HEADS, HEAD_DIM)
    grad_probs = jnp.einsum("thd,shd->hts", grad_out, values, preferred_element_type=jnp.float32)
    grad_values = jnp.einsum(
        "hts,thd->shd", probs_half, grad_out, preferred_element_type=jnp.float32
    ).astype(jnp.bfloat16)
    grad_scores = attn_probs * (
        grad_probs - jnp.sum(attn_probs * grad_probs, axis=-1, keepdims=True)
    )
    scores_half = grad_scores.astype(jnp.bfloat16)
    grad_queries = (
        jnp.einsum("hts,shd->thd", scores_half, key_rows, preferred_element_type=jnp.float32)
        * query_scale
    ).astype(jnp.bfloat16)
    grad_keys = jnp.einsum(
        "hts,thd->shd", scores_half, queries, preferred_element_type=jnp.float32
    ).astype(jnp.bfloat16)
    grad_mixed = jnp.concatenate(
        [
            grad_queries.reshape(group_rows, D),
            grad_keys.reshape(group_rows, D),
            grad_values.reshape(group_rows, D),
        ],
        axis=1,
    )
    grad_normed = lax.dot_general(
        grad_mixed, in_weight, (((1,), (1,)), ((), ())), preferred_element_type=jnp.float32
    )
    grad_unit = grad_normed * norm_gain
    grad_rows = inv_std * (
        grad_unit
        - jnp.mean(grad_unit, axis=-1, keepdims=True)
        - unit_rows * jnp.mean(grad_unit * unit_rows, axis=-1, keepdims=True)
    )
    folded = jnp.einsum(
        "haubv,uve->habe",
        grad_scores.reshape(HEADS, WIN, WIN, WIN, WIN),
        offset_table,
        precision=lax.Precision.HIGHEST,
    )
    table_part = jnp.einsum("habe,abd->hde", folded, offset_table, precision=lax.Precision.HIGHEST)
    return (grad_rows.astype(jnp.bfloat16), table_part)


def body(tokens, cotangent, norm_gain, in_weight, out_weight, bias_table):
    offset_table = offset_hot()
    bias_full = full_bias(bias_table, offset_table)
    high_parts = lax.axis_size("ha")
    wide_parts = lax.axis_size("wa")
    rows_local, cols_local, channels = tokens.shape
    row_steps = WIN // high_parts
    col_steps = WIN // wide_parts
    stride_h = rows_local // row_steps
    stride_w = cols_local // col_steps
    row_groups = stride_h // high_parts
    col_groups = stride_w // wide_parts
    group_count = row_groups * col_groups

    def to_layout(tile_block):
        laid = tile_block.reshape(
            row_steps, high_parts, row_groups, col_steps, wide_parts, col_groups, channels
        )
        laid = laid.transpose(2, 5, 1, 4, 0, 3, 6)
        return laid.reshape(group_count, high_parts, wide_parts, row_steps, col_steps, channels)

    def one_group(pair_rows):
        return group_grad(
            pair_rows[0], pair_rows[1], norm_gain, in_weight, out_weight, bias_full, offset_table
        )

    laid_tokens = to_layout(tokens)
    laid_cot = to_layout(cotangent)

    def swap_rows(laid):
        items = laid.shape[0]
        shaped = laid.reshape(items, high_parts, wide_parts, row_steps, col_steps, channels)
        return shaped.transpose(0, 1, 3, 2, 4, 5).reshape(items, WIN * WIN, channels)

    flat_shape = (group_count, high_parts * wide_parts, row_steps * col_steps, channels)
    grad_rows, table_parts = lax.map(
        one_group,
        (
            swap_rows(
                lax.all_to_all(
                    laid_tokens.reshape(flat_shape),
                    ("ha", "wa"),
                    split_axis=1,
                    concat_axis=1,
                    tiled=True,
                )
            ),
            swap_rows(
                lax.all_to_all(
                    laid_cot.reshape(flat_shape),
                    ("ha", "wa"),
                    split_axis=1,
                    concat_axis=1,
                    tiled=True,
                )
            ),
        ),
    )
    items = grad_rows.shape[0]
    shaped = grad_rows.reshape(items, high_parts, row_steps, wide_parts, col_steps, channels)
    grads_laid, table_parts = (
        shaped.transpose(0, 1, 3, 2, 4, 5).reshape(
            items, high_parts * wide_parts, row_steps * col_steps, channels
        ),
        table_parts,
    )
    returned = lax.all_to_all(grads_laid, ("ha", "wa"), split_axis=1, concat_axis=1, tiled=True)
    returned = returned.reshape(group_count, high_parts, wide_parts, row_steps, col_steps, channels)
    shaped = returned.reshape(
        row_groups, col_groups, high_parts, wide_parts, row_steps, col_steps, channels
    )
    shaped = shaped.transpose(4, 2, 0, 5, 3, 1, 6)
    grad_input = shaped.reshape(rows_local, cols_local, channels)
    grad_table = lax.psum(jnp.sum(table_parts, axis=0), ("ha", "wa"))
    return (grad_input, grad_table)


def solution(mesh):
    in_specs = (P("ha", "wa", None), P("ha", "wa", None), P(), P(), P(), P())
    out_specs = (P("ha", "wa", None), P())
    return jax.shard_map(body, mesh=mesh, in_specs=in_specs, out_specs=out_specs, check_vma=False)
```

profile of v0, /device:TPU:0, one launch (start us, length us, event | category | flops | bytes accessed | tf_op | source)
XLA Modules:
  0.0 297.9 jit_solution(12434206811364079256)
XLA Ops:
  0.6 1.3 reshape.100
  1.9 1.4 copy.57
  3.3 7.3 %all-to-all-start = ((bf16[2,32,8,512]{3,0,2,1:T(2,128)(2,1)}), bf16[2,32,8,512]{3,0,2,1:T(2,128)(2,1)S(1)}, u32[]{:S(2)}, u32[]{:S(2)}) async-start(bf16[2,32,8,512]{3,0,2,1:T(2,128)(2,1)} %bitcast.1), calls=%async_computation | async-start | bytes 1048576 | tf_op jit(solution)/shard_map/all_to_all | solution.py:142
  11.3 1.2 reshape.104
  12.6 1.4 copy.61
  15.0 11.9 %all-to-all-done = bf16[2,32,8,512]{3,0,2,1:T(2,128)(2,1)S(1)} async-done(((bf16[2,32,8,512]{3,0,2,1:T(2,128)(2,1)}), bf16[2,32,8,512]{3,0,2,1:T(2,128)(2,1)S(1)}, u32[]{:S(2)}, u32[]{:S(2)}) %all-to-all-start) | async-done | bytes 524320 | tf_op jit(solution)/shard_map/all_to_all | solution.py:142
  26.9 3.3 %all-to-all-start.1 = ((bf16[2,32,8,512]{3,0,2,1:T(2,128)(2,1)}), bf16[2,32,8,512]{3,0,2,1:T(2,128)(2,1)}, u32[]{:S(2)}, u32[]{:S(2)}) async-start(bf16[2,32,8,512]{3,0,2,1:T(2,128)(2,1)} %bitcast.14), calls=%async_computation.1 | async-start | bytes 1048576 | tf_op jit(solution)/shard_map/all_to_all | solution.py:151
  30.2 17.4 %convolution_bitcast_fusion = f32[16,16,16,16,16]{4,3,2,1,0:T(8,128)} fusion(f32[16,16,16,31]{3,1,0,2:T(8,128)S(1)} %fusion.54, s32[16,16]{1,0:T(8,128)S(1)} %copy.59), kind=kOutput, calls=%fused_computation.64 | convolution fusion | flops 390078208 | bytes 4703232 | tf_op jit(solution)/shard_map/uve,habe->haubv/dot_general | solution.py:28
  47.6 23.5 %reshape.103 = f32[16,256,256]{2,1,0:T(8,128)} reshape(f32[16,16,16,16,16]{4,3,2,1,0:T(8,128)} %convolution_bitcast_fusion) | data formatting | bytes 8388608 | tf_op jit(solution)/shard_map/reshape | solution.py:31
  71.1 5.4 %copy.64 = f32[16,256,256]{1,2,0:T(8,128)} copy(f32[16,256,256]{2,1,0:T(8,128)} %reshape.103) | data formatting | bytes 8388608
  77.2 1.6 copy.62
  79.7 162.9 %while.14 = (s32[]{:T(128)}, bf16[2,256,512]{2,1,0:T(8,128)(2,1)}, f32[2,16,31,31]{2,3,1,0:T(8,128)}, bf16[2,256,512]{2,1,0:T(8,128)(2,1)S(1)}, f32[512]{0:T(512...) while((s32[]{:T(128)}, bf16[2,256,512]{2,1,0:T(8,128)(2,1)}, ...), condition=%wide.region_8.9_spmd.clone.clone, body=%wide.region_0.8_spmd.clone.clone.sunk | while | flops 1734164224 | bytes 137940368 | solution.py:138
  80.2 1.3 convolution_convert_fusion.4
  87.9 2.9 convolution_add_fusion.2
  90.9 3.1 %fusion.130 = (f32[16,256]{1,0:T(8,128)S(1)}, f32[16,256,256]{1,2,0:T(8,128)}) fusion(f32[16,256,256]{1,2,0:T(8,128)S(1)} %convolution_add_fusion.2), kind=kOutput, calls=%fused_computation.77.clone.1 | output fusion | flops 2097407 | bytes 8404992 | tf_op jit(solution)/shard_map/while/body/eval_jaxpr/sub | solution.py:54
  94.0 5.2 %fusion.131 = bf16[16,32,256]{2,1,0:T(8,128)(2,1)} fusion(bf16[256,16,32]{0,2,1:T(8,128)(2,1)S(1)} %bitcast.199, f32[16,256]{1,0:T(8,128)S(1)} %get-tuple-element.261, f32[16,256,256]{1,2,0:T(8,128)} %copy-done.4), kind=kOutput, calls=%fused_computation.13.clone.1 | convolution fusion | flops 70390016 | bytes 4734976 | tf_op jit(solution)/shard_map/while/body/eval_jaxpr/hts,thd->shd/dot_general | solution.py:62
  99.2 3.2 %multiply_reduce_fusion.2 = (f32[16,256]{1,0:T(8,128)S(1)}, f32[16,256,256]{1,2,0:T(8,128)S(1)}) fusion(f32[16,256,256]{1,2,0:T(8,128)} %get-tuple-element.262, f32[16,256]{1,0:T(8,128)S(1)} %get-tuple-element.261, bf16[256,16,32]{0,2,1:T(8,128)(2,1)S(1)} %bitcast.200, bf16[256,16,32]{0,2,1:T(8,128)(2,1)S(1)} %bitcast.201), kind=kOutput, calls=%fused_computation.3.clone.1 | convolution fusion | flops 70250496 | bytes 8945664 | tf_op jit(solution)/shard_map/while/body/eval_jaxpr/thd,shd->hts/dot_general | solution.py:61
  107.1 19.4 %reshape.135 = f32[16,16,16,16,16]{2,1,4,3,0:T(8,128)} reshape(f32[16,256,256]{1,2,0:T(8,128)} %copy-done.2) | data formatting | bytes 8388608 | tf_op jit(solution)/shard_map/while/body/eval_jaxpr/reshape | solution.py:95
  126.5 30.4 %fusion.135 = f32[16,16,16,31,1]{3,1,4,2,0:T(8,128)S(1)} fusion(f32[16,16,16,16,16]{2,1,4,3,0:T(8,128)} %reshape.135, s32[16,16]{0,1:T(8,128)S(1)} %get-tuple-element.302), kind=kOutput, calls=%fused_computation.53.clone.1 | convolution fusion | flops 390086144 | bytes 4703232 | tf_op jit(solution)/shard_map/while/body/eval_jaxpr/haubv,uve->habe/dot_general | solution.py:93
  156.9 3.5 %fusion.136 = f32[2,16,31,31]{2,3,1,0:T(8,128)S(1)} fusion(f32[2,16,31,31]{2,3,1,0:T(8,128)S(1)} %copy-done.13, s32[]{:T(128)S(6)} %copy.96, f32[16,16,16,31,1]{3,1,4,2,0:T(8,128)S(1)} %fusion.135, s32[16,16]{0,1:T(8,128)S(1)} %get-tuple-element.302), kind=kOutput, calls=%fused_computation.18.clone.1 | convolution fusion | flops 47250944 | bytes 2367492 | tf_op jit(solution)/shard_map/while/body/eval_jaxpr/habe,abd->hde/dot_general | solution.py:99
  161.6 1.3 convolution_convert_fusion.4
  169.2 2.9 convolution_add_fusion.2
  172.2 3.1 %fusion.130 = (f32[16,256]{1,0:T(8,128)S(1)}, f32[16,256,256]{1,2,0:T(8,128)}) fusion(f32[16,256,256]{1,2,0:T(8,128)S(1)} %convolution_add_fusion.2), kind=kOutput, calls=%fused_computation.77.clone.1 | output fusion | flops 2097407 | bytes 8404992 | tf_op jit(solution)/shard_map/while/body/eval_jaxpr/sub | solution.py:54
  175.4 5.2 %fusion.131 = bf16[16,32,256]{2,1,0:T(8,128)(2,1)} fusion(bf16[256,16,32]{0,2,1:T(8,128)(2,1)S(1)} %bitcast.199, f32[16,256]{1,0:T(8,128)S(1)} %get-tuple-element.261, f32[16,256,256]{1,2,0:T(8,128)} %copy-done.4), kind=kOutput, calls=%fused_computation.13.clone.1 | convolution fusion | flops 70390016 | bytes 4734976 | tf_op jit(solution)/shard_map/while/body/eval_jaxpr/hts,thd->shd/dot_general | solution.py:62
  180.6 3.2 %multiply_reduce_fusion.2 = (f32[16,256]{1,0:T(8,128)S(1)}, f32[16,256,256]{1,2,0:T(8,128)S(1)}) fusion(f32[16,256,256]{1,2,0:T(8,128)} %get-tuple-element.262, f32[16,256]{1,0:T(8,128)S(1)} %get-tuple-element.261, bf16[256,16,32]{0,2,1:T(8,128)(2,1)S(1)} %bitcast.200, bf16[256,16,32]{0,2,1:T(8,128)(2,1)S(1)} %bitcast.201), kind=kOutput, calls=%fused_computation.3.clone.1 | convolution fusion | flops 70250496 | bytes 8945664 | tf_op jit(solution)/shard_map/while/body/eval_jaxpr/thd,shd->hts/dot_general | solution.py:61
  188.4 19.4 %reshape.135 = f32[16,16,16,16,16]{2,1,4,3,0:T(8,128)} reshape(f32[16,256,256]{1,2,0:T(8,128)} %copy-done.2) | data formatting | bytes 8388608 | tf_op jit(solution)/shard_map/while/body/eval_jaxpr/reshape | solution.py:95
  207.8 30.4 %fusion.135 = f32[16,16,16,31,1]{3,1,4,2,0:T(8,128)S(1)} fusion(f32[16,16,16,16,16]{2,1,4,3,0:T(8,128)} %reshape.135, s32[16,16]{0,1:T(8,128)S(1)} %get-tuple-element.302), kind=kOutput, calls=%fused_computation.53.clone.1 | convolution fusion | flops 390086144 | bytes 4703232 | tf_op jit(solution)/shard_map/while/body/eval_jaxpr/haubv,uve->habe/dot_general | solution.py:93
  238.2 3.5 %fusion.136 = f32[2,16,31,31]{2,3,1,0:T(8,128)S(1)} fusion(f32[2,16,31,31]{2,3,1,0:T(8,128)S(1)} %copy-done.13, s32[]{:T(128)S(6)} %copy.96, f32[16,16,16,31,1]{3,1,4,2,0:T(8,128)S(1)} %fusion.135, s32[16,16]{0,1:T(8,128)S(1)} %get-tuple-element.302), kind=kOutput, calls=%fused_computation.18.clone.1 | convolution fusion | flops 47250944 | bytes 2367492 | tf_op jit(solution)/shard_map/while/body/eval_jaxpr/habe,abd->hde/dot_general | solution.py:99
  242.6 1.2 reshape.107
  243.8 1.3 copy.66
  245.1 5.8 %all-to-all-start.2 = ((bf16[2,32,8,512]{3,0,2,1:T(2,128)(2,1)}), bf16[2,32,8,512]{3,0,2,1:T(2,128)(2,1)S(1)}, u32[]{:S(2)}, u32[]{:S(2)}) async-start(bf16[2,32,8,512]{3,0,2,1:T(2,128)(2,1)} %bitcast.19), calls=%async_computation.2 | async-start | bytes 1048576 | tf_op jit(solution)/shard_map/all_to_all | solution.py:169
  252.0 43.6 %psum.7 = f32[16,31,31]{1,2,0:T(8,128)S(1)} all-reduce(f32[16,31,31]{1,2,0:T(8,128)S(1)} %reduce_sum.63), channel_id=1, replica_groups=mesh['ha'=8,'wa'=4] {'ha','wa'}, use_global_device_ids=true, to_apply=%region_10.11 | all-reduce | flops 15376 | bytes 123008 | tf_op jit(solution)/shard_map/psum | solution.py:176
  (98 shorter events, 31.1 us)
Async XLA Ops:
  0.6 13.3 %copy-start = (f32[16,31,31]{2,0,1:T(8,128)S(1)}, f32[16,31,31]{2,0,1:T(8,128)}, u32[]{:S(2)}) copy-start(f32[16,31,31]{2,0,1:T(8,128)} %param.13) | copy-start | bytes 184516
  3.3 23.6 %all-to-all-start = ((bf16[2,32,8,512]{3,0,2,1:T(2,128)(2,1)}), bf16[2,32,8,512]{3,0,2,1:T(2,128)(2,1)S(1)}, u32[]{:S(2)}, u32[]{:S(2)}) async-start(bf16[2,32,8,512]{3,0,2,1:T(2,128)(2,1)} %bitcast.1), calls=%async_computation | async-start | bytes 1048576 | tf_op jit(solution)/shard_map/all_to_all | solution.py:142
  10.6 0.6 copy-start.11
  26.9 20.8 %copy-start.9 = (bf16[2,32,8,512]{3,0,2,1:T(2,128)(2,1)}, bf16[2,32,8,512]{3,0,2,1:T(2,128)(2,1)S(1)}, u32[]{:S(2)}) copy-start(bf16[2,32,8,512]{3,0,2,1:T(2,128)(2,1)S(1)} %all-to-all-done) | copy-start | bytes 1572868
  26.9 50.3 %all-to-all-start.1 = ((bf16[2,32,8,512]{3,0,2,1:T(2,128)(2,1)}), bf16[2,32,8,512]{3,0,2,1:T(2,128)(2,1)}, u32[]{:S(2)}, u32[]{:S(2)}) async-start(bf16[2,32,8,512]{3,0,2,1:T(2,128)(2,1)} %bitcast.14), calls=%async_computation.1 | async-start | bytes 1048576 | tf_op jit(solution)/shard_map/all_to_all | solution.py:151
  71.1 5.5 %copy-start.10 = (bf16[2,32,8,512]{3,0,2,1:T(2,128)(2,1)S(1)}, bf16[2,32,8,512]{3,0,2,1:T(2,128)(2,1)}, u32[]{:S(2)}) copy-start(bf16[2,32,8,512]{3,0,2,1:T(2,128)(2,1)} %copy-done.9) | copy-start | bytes 1572868
  76.6 3.1 %copy-start.5 = (bf16[512,1536]{1,0:T(8,128)(2,1)S(1)}, bf16[512,1536]{1,0:T(8,128)(2,1)}, u32[]{:S(2)}) copy-start(bf16[512,1536]{1,0:T(8,128)(2,1)} %param.11) | copy-start | bytes 4718596
  76.6 3.1 %copy-start.6 = (bf16[512,512]{1,0:T(8,128)(2,1)S(1)}, bf16[512,512]{1,0:T(8,128)(2,1)}, u32[]{:S(2)}) copy-start(bf16[512,512]{1,0:T(8,128)(2,1)} %param.12) | copy-start | bytes 1572868
  76.6 3.1 %copy-start.12 = (s32[16,16]{0,1:T(8,128)S(1)}, s32[16,16]{0,1:T(8,128)}, u32[]{:S(2)}) copy-start(s32[16,16]{0,1:T(8,128)} %copy-done.11) | copy-start | bytes 3076
  76.6 3.1 %copy-start.15 = (f32[512]{0:T(512)S(1)}, f32[512]{0:T(512)}, u32[]{:S(2)}) copy-start(f32[512]{0:T(512)} %param.10) | copy-start | bytes 6148
  90.8 3.2 %copy-start.4 = (f32[16,256,256]{1,2,0:T(8,128)}, f32[16,256,256]{1,2,0:T(8,128)S(1)}, u32[]{:S(2)}) copy-start(f32[16,256,256]{1,2,0:T(8,128)S(1)} %convolution_add_fusion.2) | copy-start | bytes 12582916 | tf_op jit(solution)/shard_map/while
  90.8 3.2 %copy-start.8 = (bf16[256,512]{0,1:T(8,128)(2,1)S(1)}, bf16[256,512]{0,1:T(8,128)(2,1)}, u32[]{:S(2)}) copy-start(bf16[256,512]{0,1:T(8,128)(2,1)} %copy.87) | copy-start | bytes 786436 | tf_op jit(solution)/shard_map/while
  99.2 3.4 %copy-start.3 = (f32[16,256,256]{1,2,0:T(8,128)S(1)}, f32[16,256,256]{1,2,0:T(8,128)}, u32[]{:S(2)}) copy-start(f32[16,256,256]{1,2,0:T(8,128)} %get-tuple-element.262) | copy-start | bytes 12582916 | tf_op jit(solution)/shard_map/while
  103.4 2.0 copy-start.2
  103.5 2.0 copy-start.16
  126.5 30.4 %copy-start.13 = (f32[2,16,31,31]{2,3,1,0:T(8,128)S(1)}, f32[2,16,31,31]{2,3,1,0:T(8,128)}, u32[]{:S(2)}) copy-start(f32[2,16,31,31]{2,3,1,0:T(8,128)} %get-tuple-element.284) | copy-start | bytes 369028 | tf_op jit(solution)/shard_map/while
  126.5 34.7 %copy-start.7 = (bf16[512,512]{1,0:T(8,128)(2,1)S(1)}, bf16[512,512]{1,0:T(8,128)(2,1)}, u32[]{:S(2)}) copy-start(bf16[512,512]{1,0:T(8,128)(2,1)} %get-tuple-element.315) | copy-start | bytes 1572868 | tf_op jit(solution)/shard_map/while
  160.4 0.8 copy-start.14
  172.2 3.2 %copy-start.4 = (f32[16,256,256]{1,2,0:T(8,128)}, f32[16,256,256]{1,2,0:T(8,128)S(1)}, u32[]{:S(2)}) copy-start(f32[16,256,256]{1,2,0:T(8,128)S(1)} %convolution_add_fusion.2) | copy-start | bytes 12582916 | tf_op jit(solution)/shard_map/while
  172.2 3.2 %copy-start.8 = (bf16[256,512]{0,1:T(8,128)(2,1)S(1)}, bf16[256,512]{0,1:T(8,128)(2,1)}, u32[]{:S(2)}) copy-start(bf16[256,512]{0,1:T(8,128)(2,1)} %copy.87) | copy-start | bytes 786436 | tf_op jit(solution)/shard_map/while
  180.6 3.4 %copy-start.3 = (f32[16,256,256]{1,2,0:T(8,128)S(1)}, f32[16,256,256]{1,2,0:T(8,128)}, u32[]{:S(2)}) copy-start(f32[16,256,256]{1,2,0:T(8,128)} %get-tuple-element.262) | copy-start | bytes 12582916 | tf_op jit(solution)/shard_map/while
  184.8 2.0 copy-start.2
  184.8 2.0 copy-start.16
  207.8 30.4 %copy-start.13 = (f32[2,16,31,31]{2,3,1,0:T(8,128)S(1)}, f32[2,16,31,31]{2,3,1,0:T(8,128)}, u32[]{:S(2)}) copy-start(f32[2,16,31,31]{2,3,1,0:T(8,128)} %get-tuple-element.284) | copy-start | bytes 369028 | tf_op jit(solution)/shard_map/while
  207.8 34.7 %copy-start.7 = (bf16[512,512]{1,0:T(8,128)(2,1)S(1)}, bf16[512,512]{1,0:T(8,128)(2,1)}, u32[]{:S(2)}) copy-start(bf16[512,512]{1,0:T(8,128)(2,1)} %get-tuple-element.315) | copy-start | bytes 1572868 | tf_op jit(solution)/shard_map/while
  241.7 0.8 copy-start.14
  242.5 55.3 %copy-start.1 = (f32[16,31,31]{2,0,1:T(8,128)S(1)}, f32[16,31,31]{2,0,1:T(8,128)}, u32[]{:S(2)}) copy-start(f32[16,31,31]{2,0,1:T(8,128)} %param.13) | copy-start | bytes 184516
  245.1 51.4 %all-to-all-start.2 = ((bf16[2,32,8,512]{3,0,2,1:T(2,128)(2,1)}), bf16[2,32,8,512]{3,0,2,1:T(2,128)(2,1)S(1)}, u32[]{:S(2)}, u32[]{:S(2)}) async-start(bf16[2,32,8,512]{3,0,2,1:T(2,128)(2,1)} %bitcast.19), calls=%async_computation.2 | async-start | bytes 1048576 | tf_op jit(solution)/shard_map/all_to_all | solution.py:169
where the time goes:
time: 300 us; the launch traced here: 298 us
  matrix products  117 us (39%)
  local copies, waits for them, and re-layouts  95.3 us (32%)
  blocking collectives  43.6 us (15%)
  starting transfers between devices  16.4 us (5%)
  other arithmetic  12.9 us (4%)
  waiting for transfers between devices  11.9 us (4%)
    dot_general x2, matrix products, group_grad(): jnp.einsum('haubv,uve->habe', grad_scores.reshape(HEADS, WIN, WIN, WIN, W...  60.8 us
    psum x1, blocking collectives, body(): grad_table = lax.psum(jnp.sum(table_parts, axis=0), ('ha', 'wa'))  43.6 us
    reshape x2, local copies, waits for them, and re-layouts, group_grad(): grad_scores.reshape(HEADS, WIN, WIN, WIN, WIN)  38.8 us
    reshape x1, local copies, waits for them, and re-layouts, full_bias(): return spread.reshape(HEADS, WIN * WIN, WIN * WIN)  23.5 us
    dot_general x1, matrix products, full_bias(): jnp.einsum('uve,habe->haubv', offset_table, partial_rows, precision=lax.P...  17.4 us
    all_to_all x1, waiting for transfers between devices, body(): lax.all_to_all(laid_tokens.reshape(flat_shape), ('ha', 'wa'), split_axis=...  11.9 us
    dot_general x2, matrix products, group_grad(): jnp.einsum('hts,thd->shd', probs_half, grad_out, preferred_element_type=j...  10.3 us
    unnamed x23, local copies, waits for them, and re-layouts  8.99 us
  transfers between devices with their start and end apart: 3, of which 1 were waited for; matrix products, arithmetic and copies ran while one was open for 18% of the time, Pallas kernels for 0%

commit v1 on v0

v1 whole, which is shorter than its diff:
```python
import functools

import jax
import jax.numpy as jnp
from jax import lax
from jax.experimental import pallas as pl
from jax.experimental.pallas import tpu as pltpu
from jax.sharding import PartitionSpec as P

D = 512
HEADS = 16
HEAD_DIM = 32
WIN = 16
TAB = 31
ROWS = WIN * WIN
SPAN = 2 * ROWS
LANES = 128
PER_BLOCK = LANES // HEAD_DIM
NORM_EPS = 1e-05
SCALE = HEAD_DIM ** (-0.5)


def nt(a, b):
    return lax.dot_general(a, b, (((1,), (1,)), ((), ())), preferred_element_type=jnp.float32)


def nn(a, b):
    return jnp.dot(a, b, preferred_element_type=jnp.float32)


def skew(rows, sign):
    at_row = lax.broadcasted_iota(jnp.int32, rows.shape, 0)
    for bit in range(4):
        moved = pltpu.roll(rows, (sign * (1 << bit)) % SPAN, 1)
        rows = jnp.where((at_row >> bit) % 2 == 1, moved, rows)
    return rows


def low_half():
    return lax.broadcasted_iota(jnp.int32, (WIN, SPAN), 1) % (2 * WIN) < WIN


def build_bias(tab_ref, bias_ref):
    def head(h, carry):
        pair = tab_ref[h]
        even = skew(jnp.broadcast_to(pair[0:1], (WIN, SPAN)), 1)
        odd = skew(jnp.broadcast_to(pair[1:2], (WIN, SPAN)), 1)
        strip = jnp.where(low_half(), pltpu.roll(even, SPAN - WIN, 1), odd)
        for low in range(8):
            turned = strip if low == 0 else pltpu.roll(strip, SPAN - low * WIN, 1)
            for high in range(2):
                a = WIN - 1 - (8 * high + low)
                bias_ref[h, a * WIN : (a + 1) * WIN, :] = turned[:, high * LANES : high * LANES + ROWS]
        return carry

    lax.fori_loop(0, HEADS, head, 0)


def fold_table(dsum_ref, out_ref):
    def head(h, carry):
        total = jnp.zeros((WIN, SPAN), jnp.float32)
        gap = jnp.zeros((WIN, LANES), jnp.float32)
        for low in range(8):
            first = WIN - 1 - low
            second = first - 8
            near = dsum_ref[h, first * WIN : (first + 1) * WIN, :]
            far = dsum_ref[h, second * WIN : (second + 1) * WIN, :]
            both = jnp.concatenate([near, gap, gap], axis=1) + jnp.concatenate([gap, far, gap], axis=1)
            total = total + (both if low == 0 else pltpu.roll(both, low * WIN, 1))
        low_lanes = low_half()
        even = skew(pltpu.roll(jnp.where(low_lanes, total, 0.0), WIN, 1), -1)
        odd = skew(jnp.where(low_lanes, 0.0, total), -1)
        out_ref[h] = jnp.concatenate(
            [jnp.sum(even, axis=0, keepdims=True), jnp.sum(odd, axis=0, keepdims=True)], axis=0
        )
        return carry

    lax.fori_loop(0, HEADS, head, 0)


def prepare(g, tok, cot, gain, win_ref, wout_ref, s):
    wide = tok.astype(jnp.float32)
    shifted = wide - jnp.mean(wide, axis=-1, keepdims=True)
    inv_std = lax.rsqrt(jnp.mean(shifted * shifted, axis=-1, keepdims=True) + NORM_EPS)
    unit = shifted * inv_std
    s.unit[g] = unit
    s.inv[g] = inv_std
    normed = (unit * gain).astype(jnp.bfloat16)
    queries = (nn(normed, win_ref[:, :D]) * SCALE).astype(jnp.bfloat16)
    s.q[g] = queries
    s.qt[g] = queries.T
    keys = nn(normed, win_ref[:, D : 2 * D]).astype(jnp.bfloat16)
    s.k[g] = keys
    s.kt[g] = keys.T
    s.v[g] = nn(normed, win_ref[:, 2 * D :]).astype(jnp.bfloat16)
    grad_out = nt(cot, wout_ref[...]).astype(jnp.bfloat16)
    s.o[g] = grad_out
    s.ot[g] = grad_out.T


def attend(g, s):
    lane = lax.broadcasted_iota(jnp.int32, (ROWS, LANES), 1) // HEAD_DIM

    def block(i, carry):
        at = pl.ds(pl.multiple_of(i * LANES, LANES), LANES)
        q, k, v, o = s.q[g, :, at], s.k[g, :, at], s.v[g, :, at], s.o[g, :, at]
        for j in range(PER_BLOCK):
            h = i * PER_BLOCK + j
            own = lane == j
            zero = jnp.zeros_like(q)
            scores = nt(jnp.where(own, q, zero), k) + s.bias[h]
            exponent = jnp.exp(scores - jnp.max(scores, axis=-1, keepdims=True))
            probs = exponent * (1.0 / jnp.sum(exponent, axis=-1, keepdims=True))
            grad_probs = nt(jnp.where(own, o, zero), v)
            mean = jnp.sum(probs * grad_probs, axis=-1, keepdims=True)
            grad_scores = probs * (grad_probs - mean)
            if g == 0:
                s.dsum[h] = grad_scores
            else:
                s.dsum[h] += grad_scores
            half = grad_scores.astype(jnp.bfloat16)
            rows = pl.ds(pl.multiple_of(h * HEAD_DIM, HEAD_DIM), HEAD_DIM)
            rows_k = pl.ds(pl.multiple_of(D + h * HEAD_DIM, HEAD_DIM), HEAD_DIM)
            rows_v = pl.ds(pl.multiple_of(2 * D + h * HEAD_DIM, HEAD_DIM), HEAD_DIM)
            s.mixed[rows_v, :] = nn(s.ot[g, rows, :], probs.astype(jnp.bfloat16)).astype(jnp.bfloat16)
            s.mixed[rows_k, :] = nn(s.qt[g, rows, :], half).astype(jnp.bfloat16)
            s.mixed[rows, :] = (nt(s.kt[g, rows, :], half) * SCALE).astype(jnp.bfloat16)
        return carry

    lax.fori_loop(0, HEADS // PER_BLOCK, block, 0)


def finish(g, gain, win_ref, s):
    grad_unit = nn(win_ref[...], s.mixed[...]).T * gain
    unit = s.unit[g]
    inner = grad_unit - jnp.mean(grad_unit, axis=-1, keepdims=True)
    inner = inner - unit * jnp.mean(grad_unit * unit, axis=-1, keepdims=True)
    return (s.inv[g] * inner).astype(jnp.bfloat16)


class Scratch:
    NAMES = ("unit", "inv", "q", "k", "v", "o", "qt", "kt", "ot", "mixed", "bias", "dsum")

    def __init__(self, refs):
        for name, ref in zip(self.NAMES, refs):
            setattr(self, name, ref)

    @staticmethod
    def shapes(groups):
        wide = pltpu.VMEM((groups, ROWS, D), jnp.bfloat16)
        tall = pltpu.VMEM((groups, D, ROWS), jnp.bfloat16)
        square = pltpu.VMEM((HEADS, ROWS, ROWS), jnp.float32)
        return [
            pltpu.VMEM((groups, ROWS, D), jnp.float32),
            pltpu.VMEM((groups, ROWS, 1), jnp.float32),
            wide, wide, wide, wide, tall, tall, tall,
            pltpu.VMEM((3 * D, ROWS), jnp.bfloat16),
            square, square,
        ]


def local_kernel(tok_ref, cot_ref, gain_ref, win_ref, wout_ref, tab_ref, grad_ref, out_ref, *refs):
    s = Scratch(refs)
    build_bias(tab_ref, s.bias)
    gain = gain_ref[...]
    for g in range(tok_ref.shape[0]):
        prepare(g, tok_ref[g], cot_ref[g], gain, win_ref, wout_ref, s)
        attend(g, s)
        grad_ref[g] = finish(g, gain, win_ref, s)
    fold_table(s.dsum, out_ref)


def local_call(tok, cot, gain, w_in, w_out, tab):
    groups = tok.shape[0]
    whole = pl.BlockSpec(memory_space=pltpu.VMEM)
    return pl.pallas_call(
        local_kernel,
        out_shape=(
            jax.ShapeDtypeStruct(tok.shape, jnp.bfloat16),
            jax.ShapeDtypeStruct(tab.shape, jnp.float32),
        ),
        in_specs=[whole] * 6,
        out_specs=(whole, whole),
        scratch_shapes=Scratch.shapes(groups),
        compiler_params=pltpu.CompilerParams(vmem_limit_bytes=48 * 2**20),
        name="grid_attention_grad",
    )(tok, cot, gain, w_in, w_out, tab)


def pack_table(bias_table):
    turned = jnp.flip(bias_table, (1, 2))
    padded = jnp.pad(turned, ((0, 0), (0, 1), (1, 0)))
    return padded.reshape(HEADS, WIN, 2, 2 * WIN).transpose(0, 2, 1, 3).reshape(HEADS, 2, SPAN)


def unpack_table(packed):
    split = packed.reshape(HEADS, 2, WIN, 2 * WIN).transpose(0, 2, 1, 3).reshape(HEADS, 2 * WIN, 2 * WIN)
    return jnp.flip(split[:, :TAB, 1:], (1, 2))


def body(tokens, cotangent, norm_gain, in_weight, out_weight, bias_table):
    high_parts = lax.axis_size("ha")
    wide_parts = lax.axis_size("wa")
    parts = high_parts * wide_parts
    rows_local, cols_local, channels = tokens.shape
    row_steps = WIN // high_parts
    col_steps = WIN // wide_parts
    row_groups = rows_local // row_steps // high_parts
    col_groups = cols_local // col_steps // wide_parts
    groups = row_groups * col_groups

    def send(tile):
        laid = tile.reshape(row_steps, high_parts, row_groups, col_steps, wide_parts, col_groups, channels)
        laid = laid.transpose(1, 4, 2, 5, 0, 3, 6).reshape(parts, groups * row_steps * col_steps, channels)
        got = lax.all_to_all(laid, ("ha", "wa"), split_axis=0, concat_axis=0, tiled=True)
        got = got.reshape(high_parts, wide_parts, groups, row_steps, col_steps, channels)
        return got.transpose(2, 0, 3, 1, 4, 5).reshape(groups, ROWS, channels)

    def back(grads):
        laid = grads.reshape(groups, high_parts, row_steps, wide_parts, col_steps, channels)
        laid = laid.transpose(1, 3, 0, 2, 4, 5).reshape(parts, groups * row_steps * col_steps, channels)
        got = lax.all_to_all(laid, ("ha", "wa"), split_axis=0, concat_axis=0, tiled=True)
        got = got.reshape(high_parts, wide_parts, row_groups, col_groups, row_steps, col_steps, channels)
        return got.transpose(4, 0, 2, 5, 1, 3, 6).reshape(rows_local, cols_local, channels)

    grads, packed = local_call(
        send(tokens), send(cotangent), norm_gain.reshape(1, D), in_weight, out_weight, pack_table(bias_table)
    )
    pieces = packed.reshape(parts, -1)
    pieces = lax.all_to_all(pieces, ("ha", "wa"), split_axis=0, concat_axis=0, tiled=True)
    own = jnp.broadcast_to(jnp.sum(pieces, axis=0, keepdims=True), pieces.shape)
    total = lax.all_to_all(own, ("ha", "wa"), split_axis=0, concat_axis=0, tiled=True)
    return back(grads), unpack_table(total.reshape(HEADS, 2, SPAN))


def solution(mesh):
    tile = P("ha", "wa", None)
    return jax.shard_map(
        body, mesh=mesh, in_specs=(tile, tile, P(), P(), P(), P()), out_specs=(tile, P()), check_vma=False
    )
```

time: 300 us -> 126 us (0.42)
  matrix products: 117 us -> 0 us
  local copies, waits for them, and re-layouts: 95.3 us -> 13.2 us
  waiting for transfers between devices: 11.9 us -> 50.9 us
  Pallas kernels: 0 us -> 35.7 us
  blocking collectives: 43.6 us -> 9.58 us
  other arithmetic: 12.9 us -> 0.22 us
    dot_general x22 -> x0, matrix products: 117 us -> none  [the longest x2 60.8 us: group_grad(): jnp.einsum('haubv,uve->habe', grad_scores.reshape(HEADS, WIN, WIN, WIN, W...]
    reshape x9 -> x16, local copies, waits for them, and re-layouts: 70.1 us -> 7.15 us  [the longest x4 1.98 us: send(): tile.reshape(row_steps, high_parts, row_groups, col_steps, wide_parts, co...]
    psum x1 -> x0, blocking collectives: 43.6 us -> none  [body(): grad_table = lax.psum(jnp.sum(table_parts, axis=0), ('ha', 'wa'))]
    all_to_all x3 -> x4, waiting for transfers between devices: 11.9 us -> 50.9 us  [the longest x2 29.9 us: send(): lax.all_to_all(laid, ('ha', 'wa'), split_axis=0, concat_axis=0, tiled=True)]
    pallas_call x0 -> x1, Pallas kernels: none -> 35.7 us  [local_call(): pl.pallas_call(local_kernel, out_shape=(jax.ShapeDtypeStruct(tok.shape, j...]
    all_to_all x0 -> x1, blocking collectives: none -> 9.58 us  [body(): lax.all_to_all(pieces, ('ha', 'wa'), split_axis=0, concat_axis=0, tiled=T...]
    unnamed x23 -> x11, local copies, waits for them, and re-layouts: 8.99 us -> 2.15 us
    sub x2 -> x0, other arithmetic: 6.18 us -> none  [group_grad(): exponent = jnp.exp(scores - row_top)]
  transfers between devices with their start and end apart: 3 -> 4, of which waited for: 1 -> 4; matrix products, arithmetic and copies ran while one was open for 18% -> 4% of each run, Pallas kernels for 0% -> 0%
where the time goes in v1:
time: 126 us
  waiting for transfers between devices  50.9 us (40%)
  Pallas kernels  35.7 us (28%)
  starting transfers between devices  15.1 us (12%)
  local copies, waits for them, and re-layouts  13.2 us (10%)
  blocking collectives  9.58 us (8%)
    pallas_call x1, Pallas kernels, local_call(): pl.pallas_call(local_kernel, out_shape=(jax.ShapeDtypeStruct(tok.shape, j...  35.7 us
    all_to_all x2, waiting for transfers between devices, send(): lax.all_to_all(laid, ('ha', 'wa'), split_axis=0, concat_axis=0, tiled=True)  29.9 us
    all_to_all x1, waiting for transfers between devices, back(): lax.all_to_all(laid, ('ha', 'wa'), split_axis=0, concat_axis=0, tiled=True)  14.8 us
    all_to_all x2, starting transfers between devices, send(): lax.all_to_all(laid, ('ha', 'wa'), split_axis=0, concat_axis=0, tiled=True)  9.9 us
    all_to_all x1, blocking collectives, body(): lax.all_to_all(pieces, ('ha', 'wa'), split_axis=0, concat_axis=0, tiled=T...  9.58 us
    all_to_all x1, waiting for transfers between devices, body(): lax.all_to_all(own, ('ha', 'wa'), split_axis=0, concat_axis=0, tiled=True)  6.15 us
    all_to_all x1, starting transfers between devices, back(): lax.all_to_all(laid, ('ha', 'wa'), split_axis=0, concat_axis=0, tiled=True)  2.61 us
    all_to_all x1, starting transfers between devices, body(): lax.all_to_all(own, ('ha', 'wa'), split_axis=0, concat_axis=0, tiled=True)  2.57 us
  transfers between devices with their start and end apart: 4, of which 4 were waited for; matrix products, arithmetic and copies ran while one was open for 4% of the time, Pallas kernels for 0%

profile of v1, /device:TPU:0, one launch (start us, length us, event | category | flops | bytes accessed | tf_op | source)
XLA Modules:
  0.0 125.5 jit_solution(8545088258721136892)
XLA Ops:
  0.6 1.2 reshape.63
  1.9 0.3 copy.40
  2.2 0.9 reshape.64
  3.1 7.3 %all-to-all-start = ((bf16[32,16,512]{2,1,0:T(8,128)(2,1)}), bf16[32,16,512]{2,1,0:T(8,128)(2,1)S(1)}, u32[]{:S(2)}, u32[]{:S(2)}) async-start(bf16[32,16,512]{2,1,0:T(8,128)(2,1)} %reshape.64), calls=%async_computation | async-start | bytes 1048576 | tf_op jit(solution)/shard_map/all_to_all | solution.py:215
  10.4 0.2 reshape.67
  10.6 0.3 copy.39
  10.9 0.9 reshape.68
  11.8 14.8 %all-to-all-done = bf16[32,16,512]{2,1,0:T(8,128)(2,1)S(1)} async-done(((bf16[32,16,512]{2,1,0:T(8,128)(2,1)}), bf16[32,16,512]{2,1,0:T(8,128)(2,1)S(1)}, u32[]{:S(2)}, u32[]{:S(2)}) %all-to-all-start) | async-done | bytes 524320 | tf_op jit(solution)/shard_map/all_to_all | solution.py:215
  26.6 2.6 %all-to-all-start.1 = ((bf16[32,16,512]{2,1,0:T(8,128)(2,1)}), bf16[32,16,512]{2,1,0:T(8,128)(2,1)S(1)}, u32[]{:S(2)}, u32[]{:S(2)}) async-start(bf16[32,16,512]{2,1,0:T(8,128)(2,1)} %reshape.68), calls=%async_computation.1 | async-start | bytes 1048576 | tf_op jit(solution)/shard_map/all_to_all | solution.py:215
  29.4 0.1 pad.4
  29.5 0.2 copy.41
  29.7 0.2 reshape.73.tab_ref
  30.0 0.3 copy.25
  30.3 0.1 reshape.66.tok_ref
  30.4 15.1 %all-to-all-done.1 = bf16[32,16,512]{2,1,0:T(8,128)(2,1)S(1)} async-done(((bf16[32,16,512]{2,1,0:T(8,128)(2,1)}), bf16[32,16,512]{2,1,0:T(8,128)(2,1)S(1)}, u32[]{:S(2)}, u32[]{:S(2)}) %all-to-all-start.1) | async-done | bytes 524320 | tf_op jit(solution)/shard_map/all_to_all | solution.py:215
  45.6 1.1 copy.27
  46.7 1.2 reshape.70.cot_ref
  47.9 1.0 copy-done.1
  48.9 35.7 %grid_attention_grad.1 = (bf16[2,256,512]{2,1,0:T(8,128)(2,1)S(1)}, f32[16,2,512]{2,1,0:T(2,128)S(1)}) custom-call(bf16[2,256,512]{2,1,0:T(8,128)(2,1)S(1)} %reshape.66.tok_ref, bf16[2,256,512]{2,1,0:T(8,128)(2,1)S(1)} %reshape.70.cot_ref, f32[1,512]{1,0:T(1,128)S(1)} %bitcast.26, bf16[512,1536]{1,0:T(8,128)(2,1)S(1)} %copy-done, ...), custom_call_target="tpu_custom_call" | custom-call | tf_op jit(solution)/shard_map/grid_attention_grad/pallas_call | solution.py:176
  84.8 9.6 %all_to_all.31 = f32[32,1,512]{2,1,0:T(1,128)S(1)} all-to-all(f32[32,1,512]{2,1,0:T(1,128)S(1)} %all_to_all.25), channel_id=1, replica_groups=mesh['ha'=8,'wa'=4] {'ha','wa'}, dimensions={0} | all-to-all | bytes 131072 | tf_op jit(solution)/shard_map/all_to_all | solution.py:230
  94.4 0.7 broadcast_in_dim.2
  95.1 2.6 %all-to-all-start.4 = ((f32[32,1,512]{2,1,0:T(1,128)}), f32[32,1,512]{2,1,0:T(1,128)S(1)}, u32[]{:S(2)}, u32[]{:S(2)}) async-start(f32[32,1,512]{2,1,0:T(1,128)} %broadcast_in_dim.2), calls=%async_computation.4 | async-start | bytes 131072 | tf_op jit(solution)/shard_map/all_to_all | solution.py:232
  97.8 0.3 copy.38
  98.1 0.9 reshape.75
  99.0 6.1 %all-to-all-done.4 = f32[32,1,512]{2,1,0:T(1,128)S(1)} async-done(((f32[32,1,512]{2,1,0:T(1,128)}), f32[32,1,512]{2,1,0:T(1,128)S(1)}, u32[]{:S(2)}, u32[]{:S(2)}) %all-to-all-start.4) | async-done | bytes 65568 | tf_op jit(solution)/shard_map/all_to_all | solution.py:232
  105.1 2.6 %all-to-all-start.2 = ((bf16[32,16,512]{2,1,0:T(8,128)(2,1)}), bf16[32,16,512]{2,1,0:T(8,128)(2,1)S(1)}, u32[]{:S(2)}, u32[]{:S(2)}) async-start(bf16[32,16,512]{2,1,0:T(8,128)(2,1)} %reshape.75), calls=%async_computation.2 | async-start | bytes 1048576 | tf_op jit(solution)/shard_map/all_to_all | solution.py:222
  107.8 0.2 reduce.1
  108.0 0.2 copy.32
  108.3 0.8 rev.8
  109.2 14.8 %all-to-all-done.2 = bf16[32,16,512]{2,1,0:T(8,128)(2,1)S(1)} async-done(((bf16[32,16,512]{2,1,0:T(8,128)(2,1)}), bf16[32,16,512]{2,1,0:T(8,128)(2,1)S(1)}, u32[]{:S(2)}, u32[]{:S(2)}) %all-to-all-start.2) | async-done | bytes 524320 | tf_op jit(solution)/shard_map/all_to_all | solution.py:222
  124.1 0.3 copy.30
  124.4 1.1 copy.33
  (18 shorter events, 1.1 us)
Async XLA Ops:
  1.9 8.5 %copy-start.3 = (bf16[16,32,512]{2,1,0:T(8,128)(2,1)S(1)}, bf16[16,32,512]{2,1,0:T(8,128)(2,1)}, u32[]{:S(2)}) copy-start(bf16[16,32,512]{2,1,0:T(8,128)(2,1)} %param.7) | copy-start | bytes 1572868
  3.1 23.6 %all-to-all-start = ((bf16[32,16,512]{2,1,0:T(8,128)(2,1)}), bf16[32,16,512]{2,1,0:T(8,128)(2,1)S(1)}, u32[]{:S(2)}, u32[]{:S(2)}) async-start(bf16[32,16,512]{2,1,0:T(8,128)(2,1)} %reshape.64), calls=%async_computation | async-start | bytes 1048576 | tf_op jit(solution)/shard_map/all_to_all | solution.py:215
  10.6 18.6 %copy-start.4 = (f32[16,31,31]{2,0,1:T(8,128)S(1)}, f32[16,31,31]{2,0,1:T(8,128)}, u32[]{:S(2)}) copy-start(f32[16,31,31]{2,0,1:T(8,128)} %param.11) | copy-start | bytes 184516
  26.6 18.9 %all-to-all-start.1 = ((bf16[32,16,512]{2,1,0:T(8,128)(2,1)}), bf16[32,16,512]{2,1,0:T(8,128)(2,1)S(1)}, u32[]{:S(2)}, u32[]{:S(2)}) async-start(bf16[32,16,512]{2,1,0:T(8,128)(2,1)} %reshape.68), calls=%async_computation.1 | async-start | bytes 1048576 | tf_op jit(solution)/shard_map/all_to_all | solution.py:215
  30.4 17.5 %copy-start = (bf16[512,1536]{1,0:T(8,128)(2,1)S(1)}, bf16[512,1536]{1,0:T(8,128)(2,1)}, u32[]{:S(2)}) copy-start(bf16[512,1536]{1,0:T(8,128)(2,1)} %win_ref.1) | copy-start | bytes 4718596
  30.4 17.5 %copy-start.2 = (f32[512]{0:T(512)S(1)}, f32[512]{0:T(512)}, u32[]{:S(2)}) copy-start(f32[512]{0:T(512)} %param.8) | copy-start | bytes 6148
  47.9 1.0 copy-start.1
  95.1 10.1 %all-to-all-start.4 = ((f32[32,1,512]{2,1,0:T(1,128)}), f32[32,1,512]{2,1,0:T(1,128)S(1)}, u32[]{:S(2)}, u32[]{:S(2)}) async-start(f32[32,1,512]{2,1,0:T(1,128)} %broadcast_in_dim.2), calls=%async_computation.4 | async-start | bytes 131072 | tf_op jit(solution)/shard_map/all_to_all | solution.py:232
  105.1 18.9 %all-to-all-start.2 = ((bf16[32,16,512]{2,1,0:T(8,128)(2,1)}), bf16[32,16,512]{2,1,0:T(8,128)(2,1)S(1)}, u32[]{:S(2)}, u32[]{:S(2)}) async-start(bf16[32,16,512]{2,1,0:T(8,128)(2,1)} %reshape.75), calls=%async_computation.2 | async-start | bytes 1048576 | tf_op jit(solution)/shard_map/all_to_all | solution.py:222

commit v2 on v1

--- a/solution.py
+++ b/solution.py
@@ -16,8 +16,10 @@
 SPAN = 2 * ROWS
 LANES = 128
 PER_BLOCK = LANES // HEAD_DIM
+CHUNK = 8
 NORM_EPS = 1e-05
 SCALE = HEAD_DIM ** (-0.5)
+MESH = pl.DeviceIdType.MESH
 
 
 def nt(a, b):
@@ -70,9 +72,10 @@
         low_lanes = low_half()
         even = skew(pltpu.roll(jnp.where(low_lanes, total, 0.0), WIN, 1), -1)
         odd = skew(jnp.where(low_lanes, 0.0, total), -1)
-        out_ref[h] = jnp.concatenate(
-            [jnp.sum(even, axis=0, keepdims=True), jnp.sum(odd, axis=0, keepdims=True)], axis=0
-        )
+        for parity, rows in enumerate((even, odd)):
+            row = jnp.sum(rows, axis=0, keepdims=True)
+            for k in range(SPAN // LANES):
+                out_ref[2 * h + parity, k : k + 1, :] = row[:, k * LANES : (k + 1) * LANES]
         return carry
 
     lax.fori_loop(0, HEADS, head, 0)
@@ -161,6 +164,7 @@
 
 def local_kernel(tok_ref, cot_ref, gain_ref, win_ref, wout_ref, tab_ref, grad_ref, out_ref, *refs):
     s = Scratch(refs)
+    out_ref[...] = jnp.zeros_like(out_ref)
     build_bias(tab_ref, s.bias)
     gain = gain_ref[...]
     for g in range(tok_ref.shape[0]):
@@ -177,7 +181,7 @@
         local_kernel,
         out_shape=(
             jax.ShapeDtypeStruct(tok.shape, jnp.bfloat16),
-            jax.ShapeDtypeStruct(tab.shape, jnp.float32),
+            jax.ShapeDtypeStruct((2 * HEADS, 8, LANES), jnp.float32),
         ),
         in_specs=[whole] * 6,
         out_specs=(whole, whole),
@@ -187,6 +191,169 @@
     )(tok, cot, gain, w_in, w_out, tab)
 
 
+def one_hot(rows, cols, place):
+    at = place(lax.broadcasted_iota(jnp.int32, (rows, LANES), 0))
+    at = jnp.concatenate([at] * (cols // LANES), axis=1)
+    hit = at == lax.broadcasted_iota(jnp.int32, (rows, cols), 1)
+    return jnp.where(hit, 1.0, 0.0).astype(jnp.bfloat16)
+
+
+class Plan:
+    def __init__(self, high_parts, wide_parts, rows_local, cols_local):
+        self.high, self.wide, self.cols = high_parts, wide_parts, cols_local
+        self.parts = high_parts * wide_parts
+        self.row_steps, self.col_steps = WIN // high_parts, WIN // wide_parts
+        self.stride_h, self.stride_w = rows_local // self.row_steps, cols_local // self.col_steps
+        self.row_groups, self.col_groups = self.stride_h // high_parts, self.stride_w // wide_parts
+        self.groups = self.row_groups * self.col_groups
+        self.chunk = self.row_steps * self.col_steps
+
+    def fits(self):
+        return self.chunk == CHUNK and self.parts == 2 * HEADS
+
+    def local_row(self, g, at):
+        device, step = at // self.chunk, at % self.chunk
+        p, q = device // self.wide, device % self.wide
+        r, c = step // self.col_steps, step % self.col_steps
+        row = r * self.stride_h + p * self.row_groups + g // self.col_groups
+        return row * self.cols + c * self.stride_w + q * self.col_groups + g % self.col_groups
+
+    def chunk_row(self, t):
+        i, j = t // WIN, t % WIN
+        p, r = i // self.row_steps, i % self.row_steps
+        q, c = j // self.col_steps, j % self.col_steps
+        return (p * self.wide + q, r * self.col_steps + c)
+
+    def position(self, at):
+        device, step = at // self.chunk, at % self.chunk
+        i = device // self.wide * self.row_steps + step // self.col_steps
+        return i * WIN + device % self.wide * self.col_steps + step % self.col_steps
+
+    def place_local(self, at):
+        row, col = at // self.cols, at % self.cols
+        r, a = row // self.stride_h, row % self.stride_h
+        c, b = col // self.stride_w, col % self.stride_w
+        g = a % self.row_groups * self.col_groups + b % self.col_groups
+        device = a // self.row_groups * self.wide + b // self.col_groups
+        return (g * self.parts + device) * self.chunk + r * self.col_steps + c
+
+
+def fused_kernel(plan, tok_ref, cot_ref, gain_ref, win_ref, wout_ref, tab_ref, grad_ref, out_ref, *refs):
+    (send, recv, back, home, part, mine, pieces, total, send_sem, recv_sem, *rest) = refs
+    s = Scratch(rest)
+    parts, groups = plan.parts, plan.groups
+    me = lax.axis_index("ha") * plan.wide + lax.axis_index("wa")
+    tile_rows = tok_ref.shape[0]
+
+    def others(step):
+        def one(k, carry):
+            device = (me + k) % parts
+            step(device, (device // plan.wide, device % plan.wide))
+            return carry
+
+        lax.fori_loop(1, parts, one, 0)
+
+    def scatter(source, target, slot, size=None):
+        def one(device, coords):
+            pltpu.make_async_remote_copy(
+                src_ref=source(device), dst_ref=target, send_sem=send_sem.at[slot], recv_sem=recv_sem.at[slot],
+                device_id=coords, device_id_type=MESH,
+            ).start()
+
+        others(one)
+
+    def wait(ref, sem):
+        some = ref.at[pl.ds(0, parts - 1)]
+        pltpu.make_async_copy(some, some, sem).wait()
+
+    barrier = pltpu.get_barrier_semaphore()
+    others(lambda device, coords: pl.semaphore_signal(barrier, inc=1, device_id=coords, device_id_type=MESH))
+
+    for g in range(groups):
+        pick = one_hot(ROWS, tile_rows, functools.partial(plan.local_row, g))
+        tok = nn(pick, tok_ref[...]).reshape(parts, CHUNK, D)
+        cot = nn(pick, cot_ref[...]).reshape(parts, CHUNK, D)
+        send[g] = jnp.concatenate([tok, cot], axis=1).astype(jnp.bfloat16)
+        if g == 0:
+            pl.semaphore_wait(barrier, parts - 1)
+        scatter(lambda device: send.at[g, device], recv.at[g, me], g)
+
+    part[...] = jnp.zeros_like(part)
+    build_bias(tab_ref, s.bias)
+    gain = gain_ref[...]
+
+    def in_chunks(half):
+        def place(t):
+            device, step = plan.chunk_row(t)
+            return device * (2 * CHUNK) + half * CHUNK + step
+
+        return one_hot(ROWS, 2 * CHUNK * parts, place)
+
+    for g in range(groups):
+        wait(recv.at[g], recv_sem.at[g])
+        recv[g, me] = send[g, me]
+        arrived = recv[g].reshape(2 * CHUNK * parts, D)
+        tok = nn(in_chunks(0), arrived)
+        cot = nn(in_chunks(1), arrived).astype(jnp.bfloat16)
+        prepare(g, tok, cot, gain, win_ref, wout_ref, s)
+        attend(g, s)
+        grads = nn(one_hot(ROWS, ROWS, plan.position), finish(g, gain, win_ref, s)).reshape(parts, CHUNK, D)
+        back[g] = jnp.concatenate([grads[:, :, : D // 2], grads[:, :, D // 2 :]], axis=1).astype(jnp.bfloat16)
+        scatter(lambda device: back.at[g, device], home.at[g, me], groups + g)
+
+    fold_table(s.dsum, part)
+    rows_slot, all_slot = 2 * groups, 2 * groups + 1
+    scatter(lambda device: part.at[device], pieces.at[me], rows_slot)
+    wait(pieces, recv_sem.at[rows_slot])
+    pieces[me] = part[me]
+    mine[...] = jnp.sum(pieces[...], axis=0)
+    scatter(lambda device: mine, total.at[me], all_slot)
+
+    for g in range(groups):
+        wait(home.at[g], recv_sem.at[groups + g])
+        home[g, me] = back[g, me]
+    landed = home[...].reshape(groups * parts, 2 * CHUNK, D // 2).astype(jnp.float32)
+    landed = jnp.concatenate([landed[:, :CHUNK], landed[:, CHUNK:]], axis=2)
+    landed = landed.reshape(tile_rows, D).astype(jnp.bfloat16)
+    grad_ref[...] = nn(one_hot(tile_rows, tile_rows, plan.place_local), landed).astype(jnp.bfloat16)
+
+    wait(total, recv_sem.at[all_slot])
+    total[me] = mine[...]
+    out_ref[...] = total[...]
+    for g in range(groups):
+        wait(send.at[g], send_sem.at[g])
+        wait(back.at[g], send_sem.at[groups + g])
+    wait(part, send_sem.at[rows_slot])
+    wait(total, send_sem.at[all_slot])
+
+
+def fused_call(plan, tok, cot, gain, w_in, w_out, tab):
+    groups, parts = plan.groups, plan.parts
+    whole = pl.BlockSpec(memory_space=pltpu.VMEM)
+    inward = pltpu.VMEM((groups, parts, 2 * CHUNK, D), jnp.bfloat16)
+    outward = pltpu.VMEM((groups, parts, 2 * CHUNK, D // 2), jnp.bfloat16)
+    sums = pltpu.VMEM((parts, 8, LANES), jnp.float32)
+    return pl.pallas_call(
+        functools.partial(fused_kernel, plan),
+        out_shape=(
+            jax.ShapeDtypeStruct(tok.shape, jnp.bfloat16),
+            jax.ShapeDtypeStruct((parts, 8, LANES), jnp.float32),
+        ),
+        in_specs=[whole] * 6,
+        out_specs=(whole, whole),
+        scratch_shapes=[
+            inward, inward, outward, outward,
+            sums, pltpu.VMEM((8, LANES), jnp.float32), sums, sums,
+            pltpu.SemaphoreType.DMA((2 * groups + 2,)),
+            pltpu.SemaphoreType.DMA((2 * groups + 2,)),
+        ] + Scratch.shapes(groups),
+        compiler_params=pltpu.CompilerParams(
+            vmem_limit_bytes=48 * 2**20, collective_id=0, has_side_effects=True
+        ),
+        name="grid_attention_grad_exchange",
+    )(tok, cot, gain, w_in, w_out, tab)
+
+
 def pack_table(bias_table):
     turned = jnp.flip(bias_table, (1, 2))
     padded = jnp.pad(turned, ((0, 0), (0, 1), (1, 0)))
@@ -194,20 +361,22 @@
 
 
 def unpack_table(packed):
-    split = packed.reshape(HEADS, 2, WIN, 2 * WIN).transpose(0, 2, 1, 3).reshape(HEADS, 2 * WIN, 2 * WIN)
+    split = packed[:, : SPAN // LANES].reshape(HEADS, 2, WIN, 2 * WIN).transpose(0, 2, 1, 3).reshape(HEADS, 2 * WIN, 2 * WIN)
     return jnp.flip(split[:, :TAB, 1:], (1, 2))
 
 
 def body(tokens, cotangent, norm_gain, in_weight, out_weight, bias_table):
-    high_parts = lax.axis_size("ha")
-    wide_parts = lax.axis_size("wa")
-    parts = high_parts * wide_parts
     rows_local, cols_local, channels = tokens.shape
-    row_steps = WIN // high_parts
-    col_steps = WIN // wide_parts
-    row_groups = rows_local // row_steps // high_parts
-    col_groups = cols_local // col_steps // wide_parts
-    groups = row_groups * col_groups
+    plan = Plan(lax.axis_size("ha"), lax.axis_size("wa"), rows_local, cols_local)
+    shared = (norm_gain.reshape(1, D), in_weight, out_weight, pack_table(bias_table))
+    if plan.fits():
+        flat = (rows_local * cols_local, channels)
+        grads, packed = fused_call(plan, tokens.reshape(flat), cotangent.reshape(flat), *shared)
+        return grads.reshape(tokens.shape), unpack_table(packed)
+
+    high_parts, wide_parts, parts = plan.high, plan.wide, plan.parts
+    row_steps, col_steps, groups = plan.row_steps, plan.col_steps, plan.groups
+    row_groups, col_groups = plan.row_groups, plan.col_groups
 
     def send(tile):
         laid = tile.reshape(row_steps, high_parts, row_groups, col_steps, wide_parts, col_groups, channels)
@@ -223,14 +392,12 @@
         got = got.reshape(high_parts, wide_parts, row_groups, col_groups, row_steps, col_steps, channels)
         return got.transpose(4, 0, 2, 5, 1, 3, 6).reshape(rows_local, cols_local, channels)
 
-    grads, packed = local_call(
-        send(tokens), send(cotangent), norm_gain.reshape(1, D), in_weight, out_weight, pack_table(bias_table)
-    )
+    grads, packed = local_call(send(tokens), send(cotangent), *shared)
     pieces = packed.reshape(parts, -1)
     pieces = lax.all_to_all(pieces, ("ha", "wa"), split_axis=0, concat_axis=0, tiled=True)
     own = jnp.broadcast_to(jnp.sum(pieces, axis=0, keepdims=True), pieces.shape)
     total = lax.all_to_all(own, ("ha", "wa"), split_axis=0, concat_axis=0, tiled=True)
-    return back(grads), unpack_table(total.reshape(HEADS, 2, SPAN))
+    return back(grads), unpack_table(total.reshape(packed.shape))
 
 
 def solution(mesh):

time: 126 us -> 72.8 us (0.58)
  waiting for transfers between devices: 50.9 us -> 0 us
  Pallas kernels: 35.7 us -> 65 us
  starting transfers between devices: 15.1 us -> 0 us
  blocking collectives: 9.58 us -> 0 us
  local copies, waits for them, and re-layouts: 13.2 us -> 6.81 us
    all_to_all x4 -> x0, waiting for transfers between devices: 50.9 us -> none  [the longest x2 29.9 us: send(): lax.all_to_all(laid, ('ha', 'wa'), split_axis=0, concat_axis=0, tiled=True)]
    pallas_call x1, Pallas kernels: 35.7 us -> 65 us  [fused_call(): pl.pallas_call(functools.partial(fused_kernel, plan), out_shape=(jax.Shap...]
    all_to_all x4 -> x0, starting transfers between devices: 15.1 us -> none  [the longest x2 9.9 us: send(): lax.all_to_all(laid, ('ha', 'wa'), split_axis=0, concat_axis=0, tiled=True)]
    all_to_all x1 -> x0, blocking collectives: 9.58 us -> none  [body(): lax.all_to_all(pieces, ('ha', 'wa'), split_axis=0, concat_axis=0, tiled=T...]
    reshape x14 -> x1, local copies, waits for them, and re-layouts: 6.83 us -> 0.13 us  [unpack_table(): packed[:, :SPAN // LANES].reshape(HEADS, 2, WIN, 2 * WIN)]
    unnamed x11, local copies, waits for them, and re-layouts: 2.15 us -> 3.92 us
    transpose x4 -> x1, local copies, waits for them, and re-layouts: 1.8 us -> 0.16 us  [unpack_table(): packed[:, :SPAN // LANES].reshape(HEADS, 2, WIN, 2 * WIN)]
  transfers between devices with their start and end apart: 4 -> 0, of which waited for: 4 -> 0; matrix products, arithmetic and copies ran while one was open for 4% -> 0% of each run, Pallas kernels for 0% -> 0%
where the time goes in v2:
time: 72.8 us; the launch traced here: 72.5 us
  Pallas kernels  65 us (89%)
  local copies, waits for them, and re-layouts  6.81 us (9%)
  between operations  0.73 us (1%)
    pallas_call x1, Pallas kernels, fused_call(): pl.pallas_call(functools.partial(fused_kernel, plan), out_shape=(jax.Shap...  65 us
    unnamed x11, local copies, waits for them, and re-layouts  3.92 us

profile of v2, /device:TPU:0, one launch (start us, length us, event | category | flops | bytes accessed | tf_op | source)
XLA Modules:
  0.0 72.5 jit_solution(2007809528742280811)
XLA Ops:
  0.6 0.0 copy-start
  0.6 0.0 copy-start.4
  0.7 1.2 %rev.7 = f32[16,31,31]{2,0,1:T(8,128)S(1)} reverse(f32[16,31,31]{2,0,1:T(8,128)} %param.11), dimensions={1,2} | reverse | bytes 123008 | tf_op jit(solution)/shard_map/jit(_flip)/rev | solution.py:358
  1.8 0.1 pad.4
  2.0 0.2 copy.11
  2.1 0.2 reshape.32.tab_ref
  2.3 0.0 copy-done
  2.3 0.0 copy-done.4
  2.3 0.0 copy-start.1
  2.3 1.0 %copy-done.1 = bf16[16,32,512]{2,1,0:T(8,128)(2,1)S(1)} copy-done((bf16[16,32,512]{2,1,0:T(8,128)(2,1)S(1)}, bf16[16,32,512]{2,1,0:T(8,128)(2,1)}, u32[]{:S(2)}) %copy-start.1) | copy-done | bytes 524312
  3.4 0.0 copy-start.2
  3.4 1.0 %copy-done.2 = bf16[16,32,512]{2,1,0:T(8,128)(2,1)S(1)} copy-done((bf16[16,32,512]{2,1,0:T(8,128)(2,1)S(1)}, bf16[16,32,512]{2,1,0:T(8,128)(2,1)}, u32[]{:S(2)}) %copy-start.2) | copy-done | bytes 524312
  4.4 0.0 copy-start.3
  4.4 1.0 %copy-done.3 = bf16[512,512]{1,0:T(8,128)(2,1)S(1)} copy-done((bf16[512,512]{1,0:T(8,128)(2,1)S(1)}, bf16[512,512]{1,0:T(8,128)(2,1)}, u32[]{:S(2)}) %copy-start.3) | copy-done | bytes 524312
  5.5 65.0 %grid_attention_grad_exchange.1 = (bf16[512,512]{1,0:T(8,128)(2,1)S(1)}, f32[32,8,128]{2,1,0:T(8,128)S(1)}) custom-call(bf16[512,512]{1,0:T(8,128)(2,1)S(1)} %bitcast.13, bf16[512,512]{1,0:T(8,128)(2,1)S(1)} %bitcast.14, f32[1,512]{1,0:T(1,128)S(1)} %bitcast.15, bf16[512,1536]{1,0:T(8,128)(2,1)S(1)} %copy-done, bf16[512,512]{1,0:T(8,128)(2,1)S(1)} %copy-done.3, ...), custom_call_target="tpu_custom_call" | custom-call | tf_op jit(solution)/shard_map/grid_attention_grad_exchange/pallas_call | solution.py:336
  70.5 0.1 reshape.34
  70.6 0.2 copy.9
  70.8 0.1 slice.8
  70.9 0.8 %rev.8 = f32[16,31,31]{2,0,1:T(8,128)} reverse(f32[16,31,31]{2,0,1:T(8,128)S(1)} %slice.8), dimensions={1,2} | reverse | bytes 123008 | tf_op jit(solution)/shard_map/jit(_flip)/rev | solution.py:365
  71.8 0.8 %copy.13 = bf16[16,32,512]{2,1,0:T(8,128)(2,1)} copy(bf16[16,32,512]{2,1,0:T(8,128)(2,1)S(1)} %bitcast.12) | data formatting | bytes 1048576
  (1 shorter events, 0.0 us)
Async XLA Ops:
  0.6 1.7 %copy-start = (bf16[512,1536]{1,0:T(8,128)(2,1)S(1)}, bf16[512,1536]{1,0:T(8,128)(2,1)}, u32[]{:S(2)}) copy-start(bf16[512,1536]{1,0:T(8,128)(2,1)} %win_ref.1) | copy-start | bytes 4718596
  0.6 1.7 %copy-start.4 = (f32[512]{0:T(512)S(1)}, f32[512]{0:T(512)}, u32[]{:S(2)}) copy-start(f32[512]{0:T(512)} %param.8) | copy-start | bytes 6148
  2.3 1.0 %copy-start.1 = (bf16[16,32,512]{2,1,0:T(8,128)(2,1)S(1)}, bf16[16,32,512]{2,1,0:T(8,128)(2,1)}, u32[]{:S(2)}) copy-start(bf16[16,32,512]{2,1,0:T(8,128)(2,1)} %param.6) | copy-start | bytes 1572868
  3.4 1.0 %copy-start.2 = (bf16[16,32,512]{2,1,0:T(8,128)(2,1)S(1)}, bf16[16,32,512]{2,1,0:T(8,128)(2,1)}, u32[]{:S(2)}) copy-start(bf16[16,32,512]{2,1,0:T(8,128)(2,1)} %param.7) | copy-start | bytes 1572868
  4.4 1.0 %copy-start.3 = (bf16[512,512]{1,0:T(8,128)(2,1)S(1)}, bf16[512,512]{1,0:T(8,128)(2,1)}, u32[]{:S(2)}) copy-start(bf16[512,512]{1,0:T(8,128)(2,1)} %wout_ref.1) | copy-start | bytes 1572868

commit v3 on v2

--- a/solution.py
+++ b/solution.py
@@ -51,34 +51,30 @@
         for low in range(8):
             turned = strip if low == 0 else pltpu.roll(strip, SPAN - low * WIN, 1)
             for high in range(2):
-                a = WIN - 1 - (8 * high + low)
-                bias_ref[h, a * WIN : (a + 1) * WIN, :] = turned[:, high * LANES : high * LANES + ROWS]
+                b = WIN - 1 - (8 * high + low)
+                bias_ref[h, b * WIN : (b + 1) * WIN, :] = turned[:, high * LANES : high * LANES + ROWS]
         return carry
 
     lax.fori_loop(0, HEADS, head, 0)
 
 
-def fold_table(dsum_ref, out_ref):
-    def head(h, carry):
-        total = jnp.zeros((WIN, SPAN), jnp.float32)
-        gap = jnp.zeros((WIN, LANES), jnp.float32)
-        for low in range(8):
-            first = WIN - 1 - low
-            second = first - 8
-            near = dsum_ref[h, first * WIN : (first + 1) * WIN, :]
-            far = dsum_ref[h, second * WIN : (second + 1) * WIN, :]
-            both = jnp.concatenate([near, gap, gap], axis=1) + jnp.concatenate([gap, far, gap], axis=1)
-            total = total + (both if low == 0 else pltpu.roll(both, low * WIN, 1))
-        low_lanes = low_half()
-        even = skew(pltpu.roll(jnp.where(low_lanes, total, 0.0), WIN, 1), -1)
-        odd = skew(jnp.where(low_lanes, 0.0, total), -1)
-        for parity, rows in enumerate((even, odd)):
-            row = jnp.sum(rows, axis=0, keepdims=True)
-            for k in range(SPAN // LANES):
-                out_ref[2 * h + parity, k : k + 1, :] = row[:, k * LANES : (k + 1) * LANES]
-        return carry
-
-    lax.fori_loop(0, HEADS, head, 0)
+def fold_head(h, dsum_ref, out_ref):
+    total = jnp.zeros((WIN, SPAN), jnp.float32)
+    gap = jnp.zeros((WIN, LANES), jnp.float32)
+    for low in range(8):
+        first = WIN - 1 - low
+        second = first - 8
+        near = dsum_ref[h, first * WIN : (first + 1) * WIN, :]
+        far = dsum_ref[h, second * WIN : (second + 1) * WIN, :]
+        both = jnp.concatenate([near, gap, gap], axis=1) + jnp.concatenate([gap, far, gap], axis=1)
+        total = total + (both if low == 0 else pltpu.roll(both, low * WIN, 1))
+    low_lanes = low_half()
+    even = skew(pltpu.roll(jnp.where(low_lanes, total, 0.0), WIN, 1), -1)
+    odd = skew(jnp.where(low_lanes, 0.0, total), -1)
+    for parity, rows in enumerate((even, odd)):
+        row = jnp.sum(rows, axis=0, keepdims=True)
+        for k in range(SPAN // LANES):
+            out_ref[2 * h + parity, k : k + 1, :] = row[:, k * LANES : (k + 1) * LANES]
 
 
 def prepare(g, tok, cot, gain, win_ref, wout_ref, s):
@@ -101,40 +97,47 @@
     s.ot[g] = grad_out.T
 
 
-def attend(g, s):
+def attend(g, last, s, table_ref):
     lane = lax.broadcasted_iota(jnp.int32, (ROWS, LANES), 1) // HEAD_DIM
 
     def block(i, carry):
         at = pl.ds(pl.multiple_of(i * LANES, LANES), LANES)
         q, k, v, o = s.q[g, :, at], s.k[g, :, at], s.v[g, :, at], s.o[g, :, at]
+        qt, ot = s.qt[g, at, :], s.ot[g, at, :]
+        zero = jnp.zeros_like(q)
         for j in range(PER_BLOCK):
             h = i * PER_BLOCK + j
             own = lane == j
-            zero = jnp.zeros_like(q)
-            scores = nt(jnp.where(own, q, zero), k) + s.bias[h]
-            exponent = jnp.exp(scores - jnp.max(scores, axis=-1, keepdims=True))
-            probs = exponent * (1.0 / jnp.sum(exponent, axis=-1, keepdims=True))
-            grad_probs = nt(jnp.where(own, o, zero), v)
-            mean = jnp.sum(probs * grad_probs, axis=-1, keepdims=True)
+            scores = nn(jnp.where(own, k, zero), qt) + s.bias[h]
+            exponent = jnp.exp(scores - jnp.max(scores, axis=0, keepdims=True))
+            probs = exponent * (1.0 / jnp.sum(exponent, axis=0, keepdims=True))
+            grad_probs = nn(jnp.where(own, v, zero), ot)
+            mean = jnp.sum(probs * grad_probs, axis=0, keepdims=True)
             grad_scores = probs * (grad_probs - mean)
             if g == 0:
                 s.dsum[h] = grad_scores
             else:
                 s.dsum[h] += grad_scores
             half = grad_scores.astype(jnp.bfloat16)
+            s.probs[:, j * ROWS : (j + 1) * ROWS] = probs.astype(jnp.bfloat16)
+            s.grads[:, j * ROWS : (j + 1) * ROWS] = half
+            s.own_o[j * ROWS : (j + 1) * ROWS, :] = jnp.where(own, o, zero)
+            s.own_q[j * ROWS : (j + 1) * ROWS, :] = jnp.where(own, q, zero)
             rows = pl.ds(pl.multiple_of(h * HEAD_DIM, HEAD_DIM), HEAD_DIM)
-            rows_k = pl.ds(pl.multiple_of(D + h * HEAD_DIM, HEAD_DIM), HEAD_DIM)
-            rows_v = pl.ds(pl.multiple_of(2 * D + h * HEAD_DIM, HEAD_DIM), HEAD_DIM)
-            s.mixed[rows_v, :] = nn(s.ot[g, rows, :], probs.astype(jnp.bfloat16)).astype(jnp.bfloat16)
-            s.mixed[rows_k, :] = nn(s.qt[g, rows, :], half).astype(jnp.bfloat16)
-            s.mixed[rows, :] = (nt(s.kt[g, rows, :], half) * SCALE).astype(jnp.bfloat16)
+            s.mixed_q[rows, :] = (nn(s.kt[g, rows, :], half) * SCALE).astype(jnp.bfloat16)
+            if last:
+                fold_head(h, s.dsum, table_ref)
+        at_v = pl.ds(pl.multiple_of(D + i * LANES, LANES), LANES)
+        s.mixed[:, at] = nn(s.grads[...], s.own_q[...]).astype(jnp.bfloat16)
+        s.mixed[:, at_v] = nn(s.probs[...], s.own_o[...]).astype(jnp.bfloat16)
         return carry
 
     lax.fori_loop(0, HEADS // PER_BLOCK, block, 0)
 
 
 def finish(g, gain, win_ref, s):
-    grad_unit = nn(win_ref[...], s.mixed[...]).T * gain
+    grad_normed = nt(s.mixed_q[...].T, win_ref[:, :D]) + nt(s.mixed[...], win_ref[:, D:])
+    grad_unit = grad_normed * gain
     unit = s.unit[g]
     inner = grad_unit - jnp.mean(grad_unit, axis=-1, keepdims=True)
     inner = inner - unit * jnp.mean(grad_unit * unit, axis=-1, keepdims=True)
@@ -142,7 +145,8 @@
 
 
 class Scratch:
-    NAMES = ("unit", "inv", "q", "k", "v", "o", "qt", "kt", "ot", "mixed", "bias", "dsum")
+    NAMES = ("unit", "inv", "q", "k", "v", "o", "qt", "kt", "ot", "mixed", "mixed_q",
+             "probs", "grads", "own_o", "own_q", "bias", "dsum")
 
     def __init__(self, refs):
         for name, ref in zip(self.NAMES, refs):
@@ -157,7 +161,12 @@
             pltpu.VMEM((groups, ROWS, D), jnp.float32),
             pltpu.VMEM((groups, ROWS, 1), jnp.float32),
             wide, wide, wide, wide, tall, tall, tall,
-            pltpu.VMEM((3 * D, ROWS), jnp.bfloat16),
+            pltpu.VMEM((ROWS, 2 * D), jnp.bfloat16),
+            pltpu.VMEM((D, ROWS), jnp.bfloat16),
+            pltpu.VMEM((ROWS, PER_BLOCK * ROWS), jnp.bfloat16),
+            pltpu.VMEM((ROWS, PER_BLOCK * ROWS), jnp.bfloat16),
+            pltpu.VMEM((PER_BLOCK * ROWS, LANES), jnp.bfloat16),
+            pltpu.VMEM((PER_BLOCK * ROWS, LANES), jnp.bfloat16),
             square, square,
         ]
 
@@ -169,9 +178,8 @@
     gain = gain_ref[...]
     for g in range(tok_ref.shape[0]):
         prepare(g, tok_ref[g], cot_ref[g], gain, win_ref, wout_ref, s)
-        attend(g, s)
+        attend(g, g == tok_ref.shape[0] - 1, s, out_ref)
         grad_ref[g] = finish(g, gain, win_ref, s)
-    fold_table(s.dsum, out_ref)
 
 
 def local_call(tok, cot, gain, w_in, w_out, tab):
@@ -238,8 +246,17 @@
         return (g * self.parts + device) * self.chunk + r * self.col_steps + c
 
 
-def fused_kernel(plan, tok_ref, cot_ref, gain_ref, win_ref, wout_ref, tab_ref, grad_ref, out_ref, *refs):
+def fused_kernel(plan, tok_hbm, cot_hbm, gain_ref, win_hbm, wout_hbm, tab_ref, grad_ref, out_ref, *refs):
+    tok_ref, cot_ref, win_ref, wout_ref, load_sem, *refs = refs
     (send, recv, back, home, part, mine, pieces, total, send_sem, recv_sem, *rest) = refs
+    loads = [
+        pltpu.make_async_copy(source, target, load_sem.at[k])
+        for k, (source, target) in enumerate(
+            ((tok_hbm, tok_ref), (cot_hbm, cot_ref), (win_hbm, win_ref), (wout_hbm, wout_ref))
+        )
+    ]
+    for load in loads:
+        load.start()
     s = Scratch(rest)
     parts, groups = plan.parts, plan.groups
     me = lax.axis_index("ha") * plan.wide + lax.axis_index("wa")
@@ -253,7 +270,7 @@
 
         lax.fori_loop(1, parts, one, 0)
 
-    def scatter(source, target, slot, size=None):
+    def scatter(source, target, slot):
         def one(device, coords):
             pltpu.make_async_remote_copy(
                 src_ref=source(device), dst_ref=target, send_sem=send_sem.at[slot], recv_sem=recv_sem.at[slot],
@@ -269,6 +286,8 @@
     barrier = pltpu.get_barrier_semaphore()
     others(lambda device, coords: pl.semaphore_signal(barrier, inc=1, device_id=coords, device_id_type=MESH))
 
+    loads[0].wait()
+    loads[1].wait()
     for g in range(groups):
         pick = one_hot(ROWS, tile_rows, functools.partial(plan.local_row, g))
         tok = nn(pick, tok_ref[...]).reshape(parts, CHUNK, D)
@@ -281,6 +300,9 @@
     part[...] = jnp.zeros_like(part)
     build_bias(tab_ref, s.bias)
     gain = gain_ref[...]
+    loads[2].wait()
+    loads[3].wait()
+    rows_slot, all_slot = 2 * groups, 2 * groups + 1
 
     def in_chunks(half):
         def place(t):
@@ -296,14 +318,13 @@
         tok = nn(in_chunks(0), arrived)
         cot = nn(in_chunks(1), arrived).astype(jnp.bfloat16)
         prepare(g, tok, cot, gain, win_ref, wout_ref, s)
-        attend(g, s)
+        attend(g, g == groups - 1, s, part)
+        if g == groups - 1:
+            scatter(lambda device: part.at[device], pieces.at[me], rows_slot)
         grads = nn(one_hot(ROWS, ROWS, plan.position), finish(g, gain, win_ref, s)).reshape(parts, CHUNK, D)
         back[g] = jnp.concatenate([grads[:, :, : D // 2], grads[:, :, D // 2 :]], axis=1).astype(jnp.bfloat16)
         scatter(lambda device: back.at[g, device], home.at[g, me], groups + g)
 
-    fold_table(s.dsum, part)
-    rows_slot, all_slot = 2 * groups, 2 * groups + 1
-    scatter(lambda device: part.at[device], pieces.at[me], rows_slot)
     wait(pieces, recv_sem.at[rows_slot])
     pieces[me] = part[me]
     mine[...] = jnp.sum(pieces[...], axis=0)
@@ -330,6 +351,7 @@
 def fused_call(plan, tok, cot, gain, w_in, w_out, tab):
     groups, parts = plan.groups, plan.parts
     whole = pl.BlockSpec(memory_space=pltpu.VMEM)
+    apart = pl.BlockSpec(memory_space=pl.ANY)
     inward = pltpu.VMEM((groups, parts, 2 * CHUNK, D), jnp.bfloat16)
     outward = pltpu.VMEM((groups, parts, 2 * CHUNK, D // 2), jnp.bfloat16)
     sums = pltpu.VMEM((parts, 8, LANES), jnp.float32)
@@ -339,30 +361,30 @@
             jax.ShapeDtypeStruct(tok.shape, jnp.bfloat16),
             jax.ShapeDtypeStruct((parts, 8, LANES), jnp.float32),
         ),
-        in_specs=[whole] * 6,
+        in_specs=[apart, apart, whole, apart, apart, whole],
         out_specs=(whole, whole),
-        scratch_shapes=[
+        scratch_shapes=[pltpu.VMEM(x.shape, x.dtype) for x in (tok, cot, w_in, w_out)] + [
+            pltpu.SemaphoreType.DMA((4,)),
             inward, inward, outward, outward,
             sums, pltpu.VMEM((8, LANES), jnp.float32), sums, sums,
             pltpu.SemaphoreType.DMA((2 * groups + 2,)),
             pltpu.SemaphoreType.DMA((2 * groups + 2,)),
         ] + Scratch.shapes(groups),
         compiler_params=pltpu.CompilerParams(
-            vmem_limit_bytes=48 * 2**20, collective_id=0, has_side_effects=True
+            vmem_limit_bytes=60 * 2**20, collective_id=0, has_side_effects=True
         ),
         name="grid_attention_grad_exchange",
     )(tok, cot, gain, w_in, w_out, tab)
 
 
 def pack_table(bias_table):
-    turned = jnp.flip(bias_table, (1, 2))
-    padded = jnp.pad(turned, ((0, 0), (0, 1), (1, 0)))
+    padded = jnp.pad(bias_table, ((0, 0), (0, 1), (1, 0)))
     return padded.reshape(HEADS, WIN, 2, 2 * WIN).transpose(0, 2, 1, 3).reshape(HEADS, 2, SPAN)
 
 
 def unpack_table(packed):
     split = packed[:, : SPAN // LANES].reshape(HEADS, 2, WIN, 2 * WIN).transpose(0, 2, 1, 3).reshape(HEADS, 2 * WIN, 2 * WIN)
-    return jnp.flip(split[:, :TAB, 1:], (1, 2))
+    return split[:, :TAB, 1:]
 
 
 def body(tokens, cotangent, norm_gain, in_weight, out_weight, bias_table):

time: 72.8 us -> 62.2 us (0.85)
  Pallas kernels: 65 us -> 56.4 us
  local copies, waits for them, and re-layouts: 6.81 us -> 4.9 us
    pallas_call x1, Pallas kernels: 65 us -> 56.4 us  [fused_call(): pl.pallas_call(functools.partial(fused_kernel, plan), out_shape=(jax.Shap...]
    unnamed x11 -> x3, local copies, waits for them, and re-layouts: 3.92 us -> 0.8 us
    rev x2 -> x0, local copies, waits for them, and re-layouts: 2.02 us -> none  [the longest x1 1.18 us: pack_table(): turned = jnp.flip(bias_table, (1, 2))]
    slice x1, local copies, waits for them, and re-layouts: 0.01 us -> 0.97 us  [unpack_table(): packed[:, :SPAN // LANES].reshape(HEADS, 2, WIN, 2 * WIN)]
    pad x1, local copies, waits for them, and re-layouts: 0.13 us -> 1.07 us  [pack_table(): padded = jnp.pad(bias_table, ((0, 0), (0, 1), (1, 0)))]
where the time goes in v3:
time: 62.2 us; the launch traced here: 62 us
  Pallas kernels  56.4 us (91%)
  local copies, waits for them, and re-layouts  4.9 us (8%)
  between operations  0.68 us (1%)
    pallas_call x1, Pallas kernels, fused_call(): pl.pallas_call(functools.partial(fused_kernel, plan), out_shape=(jax.Shap...  56.4 us

profile of v3, /device:TPU:0, one launch (start us, length us, event | category | flops | bytes accessed | tf_op | source)
XLA Modules:
  0.0 62.0 jit_solution(8476930572939647953)
XLA Ops:
  0.6 1.1 %pad.4 = f32[16,32,32]{2,0,1:T(8,128)S(1)} pad(f32[16,31,31]{2,0,1:T(8,128)} %param.11, f32[]{:T(128)} %constant.2.clone.1), padding=0_0x0_1x1_0 | pad | bytes 127044 | tf_op jit(solution)/shard_map/jit(_pad)/pad | solution.py:381
  1.7 0.2 copy.11
  1.9 0.8 %reshape.32.tab_ref = f32[16,2,512]{2,1,0:T(2,128)} reshape(f32[16,2,16,32]{3,2,1,0:T(8,128)S(1)} %bitcast.13) | data formatting | bytes 131072 | tf_op jit(solution)/shard_map/reshape | solution.py:382
  2.7 56.4 %grid_attention_grad_exchange.1 = (bf16[512,512]{1,0:T(8,128)(2,1)}, f32[32,8,128]{2,1,0:T(8,128)}) custom-call(bf16[512,512]{1,0:T(8,128)(2,1)} %bitcast.17, bf16[512,512]{1,0:T(8,128)(2,1)} %bitcast.18, f32[1,512]{1,0:T(1,128)} %bitcast.19, bf16[512,1536]{1,0:T(8,128)(2,1)} %win_hbm.1, bf16[512,512]{1,0:T(8,128)(2,1)} %wout_hbm.1, ...), custom_call_target="tpu_custom_call" | custom-call | tf_op jit(solution)/shard_map/grid_attention_grad_exchange/pallas_call | solution.py:358
  59.1 0.0 copy-start
  59.1 1.0 %slice.6 = f32[32,4,128]{2,1,0:T(4,128)S(1)} slice(f32[32,8,128]{2,1,0:T(8,128)} %get-tuple-element.5), slice={[0:32], [0:4], [0:128]} | slice | bytes 131072 | tf_op jit(solution)/shard_map/slice | solution.py:386
  60.1 0.1 reshape.34
  60.2 0.2 copy.9
  60.4 0.8 %slice.8 = f32[16,31,31]{2,0,1:T(8,128)} slice(f32[16,32,32]{2,0,1:T(8,128)S(1)} %bitcast.15), slice={[0:16], [0:31], [1:32]} | slice | bytes 123008 | tf_op jit(solution)/shard_map/slice | solution.py:387
  61.2 0.0 copy-done
  61.2 0.8 %copy.13 = bf16[16,32,512]{2,1,0:T(8,128)(2,1)} copy(bf16[16,32,512]{2,1,0:T(8,128)(2,1)S(1)} %bitcast.16) | data formatting | bytes 1048576
Async XLA Ops:
  59.1 2.1 %copy-start = (bf16[512,512]{1,0:T(8,128)(2,1)S(1)}, bf16[512,512]{1,0:T(8,128)(2,1)}, u32[]{:S(2)}) copy-start(bf16[512,512]{1,0:T(8,128)(2,1)} %get-tuple-element.4) | copy-start | bytes 1572868

commit v4 on v3

--- a/solution.py
+++ b/solution.py
@@ -17,6 +17,7 @@
 LANES = 128
 PER_BLOCK = LANES // HEAD_DIM
 CHUNK = 8
+STRIDE = 13
 NORM_EPS = 1e-05
 SCALE = HEAD_DIM ** (-0.5)
 MESH = pl.DeviceIdType.MESH
@@ -248,6 +249,7 @@
 
 def fused_kernel(plan, tok_hbm, cot_hbm, gain_ref, win_hbm, wout_hbm, tab_ref, grad_ref, out_ref, *refs):
     tok_ref, cot_ref, win_ref, wout_ref, load_sem, *refs = refs
+    pick_tok, pick_cot, pick_back, pick_home, *refs = refs
     (send, recv, back, home, part, mine, pieces, total, send_sem, recv_sem, *rest) = refs
     loads = [
         pltpu.make_async_copy(source, target, load_sem.at[k])
@@ -264,7 +266,7 @@
 
     def others(step):
         def one(k, carry):
-            device = (me + k) % parts
+            device = (me + STRIDE * k) % parts
             step(device, (device // plan.wide, device % plan.wide))
             return carry
 
@@ -288,6 +290,9 @@
 
     loads[0].wait()
     loads[1].wait()
+    def send_group(g):
+        scatter(lambda device: send.at[g, device], recv.at[g, me], g)
+
     for g in range(groups):
         pick = one_hot(ROWS, tile_rows, functools.partial(plan.local_row, g))
         tok = nn(pick, tok_ref[...]).reshape(parts, CHUNK, D)
@@ -295,7 +300,7 @@
         send[g] = jnp.concatenate([tok, cot], axis=1).astype(jnp.bfloat16)
         if g == 0:
             pl.semaphore_wait(barrier, parts - 1)
-        scatter(lambda device: send.at[g, device], recv.at[g, me], g)
+            send_group(0)
 
     part[...] = jnp.zeros_like(part)
     build_bias(tab_ref, s.bias)
@@ -311,17 +316,24 @@
 
         return one_hot(ROWS, 2 * CHUNK * parts, place)
 
+    pick_tok[...] = in_chunks(0)
+    pick_cot[...] = in_chunks(1)
+    pick_back[...] = one_hot(ROWS, ROWS, plan.position)
+    pick_home[...] = one_hot(tile_rows, tile_rows, plan.place_local)
+
     for g in range(groups):
         wait(recv.at[g], recv_sem.at[g])
+        if g + 1 < groups:
+            send_group(g + 1)
         recv[g, me] = send[g, me]
         arrived = recv[g].reshape(2 * CHUNK * parts, D)
-        tok = nn(in_chunks(0), arrived)
-        cot = nn(in_chunks(1), arrived).astype(jnp.bfloat16)
+        tok = nn(pick_tok[...], arrived)
+        cot = nn(pick_cot[...], arrived).astype(jnp.bfloat16)
         prepare(g, tok, cot, gain, win_ref, wout_ref, s)
         attend(g, g == groups - 1, s, part)
         if g == groups - 1:
             scatter(lambda device: part.at[device], pieces.at[me], rows_slot)
-        grads = nn(one_hot(ROWS, ROWS, plan.position), finish(g, gain, win_ref, s)).reshape(parts, CHUNK, D)
+        grads = nn(pick_back[...], finish(g, gain, win_ref, s)).reshape(parts, CHUNK, D)
         back[g] = jnp.concatenate([grads[:, :, : D // 2], grads[:, :, D // 2 :]], axis=1).astype(jnp.bfloat16)
         scatter(lambda device: back.at[g, device], home.at[g, me], groups + g)
 
@@ -336,11 +348,11 @@
     landed = home[...].reshape(groups * parts, 2 * CHUNK, D // 2).astype(jnp.float32)
     landed = jnp.concatenate([landed[:, :CHUNK], landed[:, CHUNK:]], axis=2)
     landed = landed.reshape(tile_rows, D).astype(jnp.bfloat16)
-    grad_ref[...] = nn(one_hot(tile_rows, tile_rows, plan.place_local), landed).astype(jnp.bfloat16)
+    grad_ref[...] = nn(pick_home[...], landed).astype(jnp.bfloat16)
 
     wait(total, recv_sem.at[all_slot])
     total[me] = mine[...]
-    out_ref[...] = total[...]
+    out_ref[...] = total[:, : SPAN // LANES, :]
     for g in range(groups):
         wait(send.at[g], send_sem.at[g])
         wait(back.at[g], send_sem.at[groups + g])
@@ -359,12 +371,16 @@
         functools.partial(fused_kernel, plan),
         out_shape=(
             jax.ShapeDtypeStruct(tok.shape, jnp.bfloat16),
-            jax.ShapeDtypeStruct((parts, 8, LANES), jnp.float32),
+            jax.ShapeDtypeStruct((parts, SPAN // LANES, LANES), jnp.float32),
         ),
         in_specs=[apart, apart, whole, apart, apart, whole],
         out_specs=(whole, whole),
         scratch_shapes=[pltpu.VMEM(x.shape, x.dtype) for x in (tok, cot, w_in, w_out)] + [
             pltpu.SemaphoreType.DMA((4,)),
+            pltpu.VMEM((ROWS, 2 * CHUNK * parts), jnp.bfloat16),
+            pltpu.VMEM((ROWS, 2 * CHUNK * parts), jnp.bfloat16),
+            pltpu.VMEM((ROWS, ROWS), jnp.bfloat16),
+            pltpu.VMEM((tok.shape[0], tok.shape[0]), jnp.bfloat16),
             inward, inward, outward, outward,
             sums, pltpu.VMEM((8, LANES), jnp.float32), sums, sums,
             pltpu.SemaphoreType.DMA((2 * groups + 2,)),
@@ -383,7 +399,7 @@
 
 
 def unpack_table(packed):
-    split = packed[:, : SPAN // LANES].reshape(HEADS, 2, WIN, 2 * WIN).transpose(0, 2, 1, 3).reshape(HEADS, 2 * WIN, 2 * WIN)
+    split = packed.reshape(HEADS, 2, WIN, 2 * WIN).transpose(0, 2, 1, 3).reshape(HEADS, 2 * WIN, 2 * WIN)
     return split[:, :TAB, 1:]
 
 
@@ -419,7 +435,7 @@
     pieces = lax.all_to_all(pieces, ("ha", "wa"), split_axis=0, concat_axis=0, tiled=True)
     own = jnp.broadcast_to(jnp.sum(pieces, axis=0, keepdims=True), pieces.shape)
     total = lax.all_to_all(own, ("ha", "wa"), split_axis=0, concat_axis=0, tiled=True)
-    return back(grads), unpack_table(total.reshape(packed.shape))
+    return back(grads), unpack_table(total.reshape(packed.shape)[:, : SPAN // LANES])
 
 
 def solution(mesh):

time: 62.2 us -> 65.3 us (1.050)
  Pallas kernels: 56.4 us -> 59.6 us
    pallas_call x1, Pallas kernels: 56.4 us -> 59.6 us  [fused_call(): pl.pallas_call(functools.partial(fused_kernel, plan), out_shape=(jax.Shap...]
    slice x1 -> x0, local copies, waits for them, and re-layouts: 0.97 us -> none  [unpack_table(): packed[:, :SPAN // LANES].reshape(HEADS, 2, WIN, 2 * WIN)]
    reshape x1, local copies, waits for them, and re-layouts: 0.13 us -> 1.02 us  [unpack_table(): packed.reshape(HEADS, 2, WIN, 2 * WIN).transpose(0, 2, 1, 3)]
where the time goes in v4:
time: 65.3 us; the launch traced here: 65.1 us
  Pallas kernels  59.6 us (91%)
  local copies, waits for them, and re-layouts  4.83 us (7%)
  between operations  0.67 us (1%)
    pallas_call x1, Pallas kernels, fused_call(): pl.pallas_call(functools.partial(fused_kernel, plan), out_shape=(jax.Shap...  59.6 us

profile of v4, /device:TPU:0, one launch (start us, length us, event | category | flops | bytes accessed | tf_op | source)
XLA Modules:
  0.0 65.1 jit_solution(7601834198699480676)
XLA Ops:
  0.6 1.1 %pad.4 = f32[16,32,32]{2,0,1:T(8,128)S(1)} pad(f32[16,31,31]{2,0,1:T(8,128)} %param.11, f32[]{:T(128)} %constant.2.clone.1), padding=0_0x0_1x1_0 | pad | bytes 127044 | tf_op jit(solution)/shard_map/jit(_pad)/pad | solution.py:397
  1.7 0.2 copy.11
  1.9 0.8 %reshape.32.tab_ref = f32[16,2,512]{2,1,0:T(2,128)} reshape(f32[16,2,16,32]{3,2,1,0:T(8,128)S(1)} %bitcast.13) | data formatting | bytes 131072 | tf_op jit(solution)/shard_map/reshape | solution.py:398
  2.7 59.6 %grid_attention_grad_exchange.1 = (bf16[512,512]{1,0:T(8,128)(2,1)}, f32[32,4,128]{2,1,0:T(4,128)}) custom-call(bf16[512,512]{1,0:T(8,128)(2,1)} %bitcast.17, bf16[512,512]{1,0:T(8,128)(2,1)} %bitcast.18, f32[1,512]{1,0:T(1,128)} %bitcast.19, bf16[512,1536]{1,0:T(8,128)(2,1)} %win_hbm.1, bf16[512,512]{1,0:T(8,128)(2,1)} %wout_hbm.1, ...), custom_call_target="tpu_custom_call" | custom-call | tf_op jit(solution)/shard_map/grid_attention_grad_exchange/pallas_call | solution.py:370
  62.3 0.0 copy-start
  62.3 1.0 %reshape.34 = f32[16,2,16,32]{3,2,1,0:T(8,128)S(1)} reshape(f32[32,4,128]{2,1,0:T(4,128)} %get-tuple-element.5) | data formatting | bytes 131072 | tf_op jit(solution)/shard_map/reshape | solution.py:402
  63.3 0.2 copy.9
  63.5 0.8 %slice.4 = f32[16,31,31]{2,0,1:T(8,128)} slice(f32[16,32,32]{2,0,1:T(8,128)S(1)} %bitcast.15), slice={[0:16], [0:31], [1:32]} | slice | bytes 123008 | tf_op jit(solution)/shard_map/slice | solution.py:403
  64.3 0.0 copy-done
  64.3 0.8 %copy.13 = bf16[16,32,512]{2,1,0:T(8,128)(2,1)} copy(bf16[16,32,512]{2,1,0:T(8,128)(2,1)S(1)} %bitcast.16) | data formatting | bytes 1048576
Async XLA Ops:
  62.3 2.0 %copy-start = (bf16[512,512]{1,0:T(8,128)(2,1)S(1)}, bf16[512,512]{1,0:T(8,128)(2,1)}, u32[]{:S(2)}) copy-start(bf16[512,512]{1,0:T(8,128)(2,1)} %get-tuple-element.4) | copy-start | bytes 1572868
